TPU v7x, 256 devices: a whole 4x4x8 slice. The times are simulated.
256 devices in a mesh: img: 16 (over y_lo, x, core), slab: 16 (over z, y_hi).
Axes of the slice: x: 4, y: 4 (y_hi: 2, y_lo: 2; y = y_hi * 2 + y_lo), z: 8, core: 2. Of those that a mesh axis runs over, the one named last changes fastest.
Arguments:
- state: float32 [128, 2, 512, 4, 128], P('img', None, 'slab'), may hold values from -3 to 3
- sources: int32 [128, 2], replicated, may hold values from 0 to 127, as said below
- weight_index: int32 [128], P('img'), may hold values from 0 to 15
Outputs:
- moved: float32 [128, 2, 512, 4, 128], P('img', None, 'slab')
Inputs may be any that keep to these rules, and one draw needn't show every extreme that they name: Among the 16 sources of the 8 new images of one device (aligned blocks), at most 2 lie among the 8 images of any one device, and in every draw exactly 2 do for some devices.
All inputs are finite; a program needn't handle non-finite values.
Results may differ from a plain program's by a relative error of at most 0.00022.
Values sent between devices are 32-bit elements; how exact they have to be, the bound alone decides.
No kernel may reach another device: no remote copies, remote signals or barrier semaphores. Data moves between devices by JAX's collectives and lax.ppermute only.
A program may use at most 128 MiB of HBM per device.

v0:
```python
import jax
import jax.numpy as jnp
from jax import lax
from jax.sharding import PartitionSpec as P

WLEVELS = 16


KAPPA = 0.25
COUPLE = 0.3
STEP_SIZE = 0.004
EPSILON = 1e-06


def with_halo(block, sides, width):
    for axis, dim in sides:
        count = lax.axis_size(axis)
        forward = [(i, i + 1) for i in range(count - 1)]
        backward = [(target, source) for source, target in forward]
        low = lax.ppermute(
            lax.slice_in_dim(block, block.shape[dim] - width, None, axis=dim), axis, forward
        )
        high = lax.ppermute(lax.slice_in_dim(block, 0, width, axis=dim), axis, backward)
        block = jnp.concatenate([low, block, high], axis=dim)
    return block


def drift(phi, face):
    padded = jnp.pad(phi, ((0, 0), (1, 1), (0, 0), (0, 0)))
    lapl = padded[:, 2:] + padded[:, :-2]
    lapl = lapl + jnp.roll(phi, 1, 2) + jnp.roll(phi, -1, 2)
    lapl = lapl + jnp.roll(phi, 1, 3) + jnp.roll(phi, -1, 3) - 6.0 * phi
    potential = phi * phi * phi - phi + COUPLE * phi[::-1] - KAPPA * lapl
    mobile = 0.5 + 1.0 / (1.0 + phi * phi)
    total = jnp.zeros_like(phi)
    for axis_no in (2, 3):
        face_mob = 0.5 * (mobile + jnp.roll(mobile, -1, axis_no))
        flux = face_mob * (jnp.roll(potential, -1, axis_no) - potential)
        total = total + flux - jnp.roll(flux, 1, axis_no)
    face_z = 0.5 * (mobile[:, 1:] + mobile[:, :-1]) * face[None, :, None, None]
    flux_z = face_z * (potential[:, 1:] - potential[:, :-1])
    total = total + jnp.pad(flux_z, ((0, 0), (0, 1), (0, 0), (0, 0)))
    total = total - jnp.pad(flux_z, ((0, 0), (1, 0), (0, 0), (0, 0)))
    return total


def face_mask(zbase, total_z, depth, margin):
    rows = zbase - margin + jnp.arange(depth + 2 * margin, dtype=jnp.int32)
    inside = (rows >= 0) & (rows < total_z)
    return ((inside[1:] & inside[:-1]).astype(jnp.float32), inside)


def pull_back(window, moment, face):

    def single(pair):
        field, cotangent = pair
        _, back = jax.vjp(lambda value: drift(value, face), field)
        return back(cotangent)[0]

    return lax.map(single, (window, moment))


def all_drifts(window, face):
    return lax.map(lambda field: drift(field, face), window)


def scales(own_drift, tangent):
    drift_sq, tangent_sq = lax.psum(
        (
            jnp.sum(own_drift * own_drift, axis=(1, 2, 3, 4)),
            jnp.sum(tangent * tangent, axis=(1, 2, 3, 4)),
        ),
        "slab",
    )
    return jnp.sqrt(drift_sq) / jnp.sqrt(tangent_sq + EPSILON)


def local(state, sources, weight_index):
    count = lax.axis_size("img")
    img_rank = lax.axis_index("img")
    per_dev = state.shape[0]
    images = per_dev * count
    depth = state.shape[2]
    total_z = depth * lax.axis_size("slab")
    zbase = lax.axis_index("slab") * depth
    path = with_halo(state, (("img", 0),), 1)
    tangent = (path[2:] - path[:-2]) * ((images - 1) / 2.0)
    second = (path[2:] - 2.0 * path[1:-1] + path[:-2]) * float((images - 1) ** 2)
    window = with_halo(state, (("slab", 2),), 3)
    face, inside = face_mask(zbase, total_z, depth, 3)
    drifts = all_drifts(window, face)
    own_drift = drifts[:, :, 3:-3]
    scale = scales(own_drift, tangent)
    moment = scale[:, None, None, None, None] * tangent - own_drift
    moment_rim = with_halo(moment, (("slab", 2),), 2)
    moment_rim = jnp.pad(moment_rim, ((0, 0), (0, 0), (1, 1), (0, 0), (0, 0)))
    pulled = pull_back(window, moment_rim, face)[:, :, 3:-3]
    global_ids = img_rank * per_dev + jnp.arange(per_dev, dtype=jnp.int32)
    interior = ((global_ids > 0) & (global_ids < images - 1))[:, None, None, None, None]
    square = (scale * scale)[:, None, None, None, None]
    updated = jnp.where(interior, state + STEP_SIZE * (square * second + pulled), state)
    weights = (weight_index.astype(jnp.float32) + 1.0) / (WLEVELS + 1.0)
    mine = lax.dynamic_slice_in_dim(sources, img_rank * per_dev, per_dev, 0)
    piece = lax.all_gather(updated, "img", axis=0, tiled=True)
    number = piece.shape[0]
    image_ids = jnp.arange(number, dtype=jnp.int32)
    table = weights[:, None] * (mine[:, 0:1] == image_ids[None, :]).astype(jnp.float32)
    table = table + (1.0 - weights)[:, None] * (mine[:, 1:2] == image_ids[None, :]).astype(
        jnp.float32
    )
    flat = piece.reshape(number, -1)
    added = jnp.dot(
        table, flat, precision=lax.Precision.HIGHEST, preferred_element_type=jnp.float32
    )
    return added.reshape(jnp.zeros_like(updated).shape)


def solution(mesh):
    return jax.shard_map(
        local,
        mesh=mesh,
        in_specs=(P("img", None, "slab", None, None), P(), P("img")),
        out_specs=P("img", None, "slab", None, None),
        check_vma=False,
    )
```

profile of v0, /device:TPU:1, one launch (start us, length us, event | category | flops | bytes accessed | tf_op | source)
XLA Modules:
  0.0 294.0 jit_solution(5869234508905326577)
XLA Ops:
  6.5 1.4 copy.25
  8.7 5.1 %collective-permute-start = (f32[1,2,32,4,128]{4,2,3,1,0:T(8,128)}, f32[1,2,32,4,128]{4,2,3,1,0:T(8,128)}, u32[]{:S(2)}, u32[]{:S(2)}) collective-permute-start(f32[1,2,32,4,128]{4,2,3,1,0:T(8,128)} %get-tuple-element.204), channel_id=1, source_target_pairs={{16,0},{32,16},{48,32},{64,48},{80,64},{96,80},{112,96},{128,112},... | collective-permute-start | bytes 393224 | tf_op jit(solution)/shard_map/ppermute | solution.py:23
  13.8 1.9 collective-permute-start.1
  16.4 4.2 %collective-permute-start.2 = (f32[8,2,3,4,128]{4,3,2,1,0:T(4,128)S(1)}, f32[8,2,3,4,128]{4,3,2,1,0:T(4,128)S(1)}, u32[]{:S(2)}, u32[]{:S(2)}) collective-permute-start(f32[8,2,3,4,128]{4,3,2,1,0:T(4,128)S(1)} %get-tuple-element.207), channel_id=1, source_target_pairs={{0,1},{1,2},{2,3},{3,4},{4,5},{5,6},{6,7},{7,8},{8,9},{9,10},{10,1... | collective-permute-start | bytes 294920 | tf_op jit(solution)/shard_map/ppermute | solution.py:20
  20.6 1.3 collective-permute-start.3
  22.0 1.5 collective-permute-done.2
  23.6 4.6 %collective-permute-done.3 = f32[8,2,3,4,128]{4,3,2,1,0:T(4,128)S(1)} collective-permute-done((f32[8,2,3,4,128]{4,3,2,1,0:T(4,128)}, f32[8,2,3,4,128]{4,3,2,1,0:T(4,128)S(1)}, u32[]{:S(2)}, u32[]{:S(2)}) %collective-permute-start.3) | collective-permute-done | bytes 98336 | tf_op jit(solution)/shard_map/ppermute | solution.py:23
  28.5 18.8 %while.24 = (s32[]{:T(128)}, f32[8,2,38,4,128]{4,3,2,1,0:T(4,128)S(1)}, f32[8,2,38,4,128]{4,3,2,1,0:T(4,128)S(1)}, f32[37]{0:T(128)S(1)}, s32[]{:T(128)}) while((s32[]{:T(128)}, f32[8,2,38,4,128]{4,3,2,1,0:T(4,128)S(1)}, f32[8,2,38,4,128]{4,3,2,1,0:T(4,128)S(1)}, f32[37]{0:T(128)S(1)}, s32[]{:T(128)}) %tuple.116), condition=%wide.region_1.2_spmd, body=%wide.region_0.1_spmd.sunk | while | flops 1902631 | bytes 7094401 | solution.py:64
  47.3 1.0 copy-done.2
  48.3 1.0 copy-done.3
  49.4 1.4 copy.22
  51.0 1.2 multiply_reduce_fusion
  52.3 34.7 %all-reduce.31 = (f32[8]{0:T(128)S(1)}, f32[8]{0:T(128)S(1)}) all-reduce(f32[8]{0:T(128)S(1)} %multiply_reduce_fusion, f32[8]{0:T(128)S(1)} %multiply_reduce_fusion.1), channel_id=1, replica_groups=mesh['img'=16,'slab'=16] {'slab'}, use_global_device_ids=true, to_apply=%region_5.6 | all-reduce | flops 16 | bytes 128 | tf_op jit(solution)/shard_map/psum | solution.py:68
  87.0 1.3 multiply_subtract_fusion.2
  88.3 3.3 %collective-permute-start.4 = (f32[8,2,2,4,128]{4,2,3,1,0:T(2,128)S(1)}, f32[8,2,2,4,128]{4,2,3,1,0:T(2,128)S(1)}, u32[]{:S(2)}, u32[]{:S(2)}) collective-permute-start(f32[8,2,2,4,128]{4,2,3,1,0:T(2,128)S(1)} %get-tuple-element.202), channel_id=1, source_target_pairs={{0,1},{1,2},{2,3},{3,4},{4,5},{5,6},{6,7},{7,8},{8,9},{9,10},{10,1... | collective-permute-start | bytes 196616 | tf_op jit(solution)/shard_map/ppermute | solution.py:20
  91.7 1.5 collective-permute-start.5
  93.2 5.0 %collective-permute-done.5 = f32[8,2,2,4,128]{4,2,3,1,0:T(2,128)S(1)} collective-permute-done((f32[8,2,2,4,128]{4,2,3,1,0:T(2,128)S(1)}, f32[8,2,2,4,128]{4,2,3,1,0:T(2,128)S(1)}, u32[]{:S(2)}, u32[]{:S(2)}) %collective-permute-start.5) | collective-permute-done | bytes 65568 | tf_op jit(solution)/shard_map/ppermute | solution.py:23
  99.1 40.9 %while.25 = (s32[]{:T(128)}, f32[8,2,38,4,128]{4,3,2,1,0:T(4,128)S(1)}, f32[8,2,38,4,128]{4,3,2,1,0:T(4,128)}, f32[8,2,38,4,128]{4,3,2,1,0:T(4,128)S(1)}, f32[37]{0:T(128)S(1)}, /*index=5*/s32[]{:T(128)}) while((s32[]{:T(128)}, f32[8,2,38,4,128]{4,3,2,1,0:T(4,128)S(1)}, f32[8,2,38,4,128]{4,3,2,1,0:T(4,128)}, ...), condition=%wide.region_7.8_spmd, body=%wide.region_6.7_spmd.sunk | while | flops 4076583 | bytes 13607197 | solution.py:60
  99.1 1.0 divide_add_fusion.2
  103.5 0.7 bitcast_dynamic-update-slice_fusion.2
  104.3 1.0 divide_add_fusion.2
  109.4 1.0 divide_add_fusion.2
  114.5 1.0 divide_add_fusion.2
  119.6 1.0 divide_add_fusion.2
  124.7 1.0 divide_add_fusion.2
  129.8 1.0 divide_add_fusion.2
  134.9 1.0 divide_add_fusion.2
  140.1 2.4 add_select_fusion
  142.7 107.4 %all-gather.2.cloned.1.call-done = f32[128,2,32,4,128]{4,2,3,1,0:T(8,128)} async-done(((f32[8,2,32,4,128]{4,2,3,1,0:T(8,128)}), f32[128,2,32,4,128]{4,2,3,1,0:T(8,128)}) %all-gather.2.cloned.1.call-update) | async-done | bytes 16777232 | tf_op jit(solution)/shard_map/all_gather | solution.py:104
  250.1 19.8 %copy.27 = f32[128,2,32,4,128]{0,4,3,2,1:T(8,128)} copy(f32[128,2,32,4,128]{4,2,3,1,0:T(8,128)} %all-gather.2.cloned.1.call-done) | data formatting | bytes 33554432 | tf_op jit(solution)/shard_map/all_gather | solution.py:104
  269.8 16.1 %fusion.49 = f32[8,2,32,4,128]{4,0,3,2,1:T(8,128)S(1)} fusion(f32[128,2,32,4,128]{0,4,3,2,1:T(8,128)} %copy.27, f32[8]{0:T(128)S(1)} %get-tuple-element.211, s32[8]{0:T(128)S(1)} %get-tuple-element.209, f32[8]{0:T(128)S(1)} %get-tuple-element.210, s32[8]{0:T(128)S(1)} %get-tuple-element.208), kind=kOutput, calls=%fused_computation.86 | convolution fusion | flops 402658304 | bytes 17825920 | tf_op jit(solution)/shard_map/dot_general | solution.py:112
  285.9 1.3 copy.28
  (393 shorter events, 51.5 us)
Async XLA Ops:
  6.5 136.0 %copy-start = (s32[128,2]{0,1:T(2,128)S(1)}, s32[128,2]{0,1:T(2,128)}, u32[]{:S(2)}) copy-start(s32[128,2]{0,1:T(2,128)} %param.8) | copy-start | bytes 3076
  6.5 9.2 %copy-start.1 = (f32[8,2,32,4,128]{4,3,2,1,0:T(4,128)S(1)}, f32[8,2,32,4,128]{4,3,2,1,0:T(4,128)}, u32[]{:S(2)}) copy-start(f32[8,2,32,4,128]{4,3,2,1,0:T(4,128)} %param.7) | copy-start | bytes 3145732
  6.5 243.5 %all-gather.2.cloned.1.call-start = ((), (), s32[]{:S(2)}) async-start(), calls=%async_computation | async-start | bytes 17825792 | tf_op jit(solution)/shard_map/all_gather | solution.py:104
  8.7 42.3 %collective-permute-start = (f32[1,2,32,4,128]{4,2,3,1,0:T(8,128)}, f32[1,2,32,4,128]{4,2,3,1,0:T(8,128)}, u32[]{:S(2)}, u32[]{:S(2)}) collective-permute-start(f32[1,2,32,4,128]{4,2,3,1,0:T(8,128)} %get-tuple-element.204), channel_id=1, source_target_pairs={{16,0},{32,16},{48,32},{64,48},{80,64},{96,80},{112,96},{128,112},... | collective-permute-start | bytes 393224 | tf_op jit(solution)/shard_map/ppermute | solution.py:23
  13.8 37.2 %collective-permute-start.1 = (f32[1,2,32,4,128]{4,2,3,1,0:T(8,128)}, f32[1,2,32,4,128]{4,2,3,1,0:T(8,128)}, u32[]{:S(2)}, u32[]{:S(2)}) collective-permute-start(f32[1,2,32,4,128]{4,2,3,1,0:T(8,128)} %get-tuple-element.205), channel_id=1, source_target_pairs={{0,16},{16,32},{32,48},{48,64},{64,80},{80,96},{96,112},{112,128},... | collective-permute-start | bytes 393224 | tf_op jit(solution)/shard_map/ppermute | solution.py:20
  16.4 7.0 %collective-permute-start.2 = (f32[8,2,3,4,128]{4,3,2,1,0:T(4,128)S(1)}, f32[8,2,3,4,128]{4,3,2,1,0:T(4,128)S(1)}, u32[]{:S(2)}, u32[]{:S(2)}) collective-permute-start(f32[8,2,3,4,128]{4,3,2,1,0:T(4,128)S(1)} %get-tuple-element.207), channel_id=1, source_target_pairs={{0,1},{1,2},{2,3},{3,4},{4,5},{5,6},{6,7},{7,8},{8,9},{9,10},{10,1... | collective-permute-start | bytes 294920 | tf_op jit(solution)/shard_map/ppermute | solution.py:20
  20.6 7.7 %collective-permute-start.3 = (f32[8,2,3,4,128]{4,3,2,1,0:T(4,128)}, f32[8,2,3,4,128]{4,3,2,1,0:T(4,128)S(1)}, u32[]{:S(2)}, u32[]{:S(2)}) collective-permute-start(f32[8,2,3,4,128]{4,3,2,1,0:T(4,128)} %get-tuple-element.206), channel_id=1, source_target_pairs={{1,0},{2,1},{3,2},{4,3},{5,4},{6,5},{7,6},{8,7},{9,8},{10,9},{11,1... | collective-permute-start | bytes 294920 | tf_op jit(solution)/shard_map/ppermute | solution.py:23
  47.3 1.0 copy-start.2
  48.3 1.0 copy-start.3
  88.3 4.9 %collective-permute-start.4 = (f32[8,2,2,4,128]{4,2,3,1,0:T(2,128)S(1)}, f32[8,2,2,4,128]{4,2,3,1,0:T(2,128)S(1)}, u32[]{:S(2)}, u32[]{:S(2)}) collective-permute-start(f32[8,2,2,4,128]{4,2,3,1,0:T(2,128)S(1)} %get-tuple-element.202), channel_id=1, source_target_pairs={{0,1},{1,2},{2,3},{3,4},{4,5},{5,6},{6,7},{7,8},{8,9},{9,10},{10,1... | collective-permute-start | bytes 196616 | tf_op jit(solution)/shard_map/ppermute | solution.py:20
  91.7 6.5 %collective-permute-start.5 = (f32[8,2,2,4,128]{4,2,3,1,0:T(2,128)S(1)}, f32[8,2,2,4,128]{4,2,3,1,0:T(2,128)S(1)}, u32[]{:S(2)}, u32[]{:S(2)}) collective-permute-start(f32[8,2,2,4,128]{4,2,3,1,0:T(2,128)S(1)} %get-tuple-element.203), channel_id=1, source_target_pairs={{1,0},{2,1},{3,2},{4,3},{5,4},{6,5},{7,6},{8,7},{9,8},{10,9},{11,1... | collective-permute-start | bytes 196616 | tf_op jit(solution)/shard_map/ppermute | solution.py:23
  140.1 2.5 copy-start.4
Sparse Core Ops, SparseCore 0:
  142.7 107.3 all-gather.1
where the time goes:
time: 295 us; the launch traced here: 294 us
  waiting for transfers between devices  119 us (40%)
  local copies, waits for them, and re-layouts  51.6 us (17%)
  other arithmetic  39.7 us (13%)
  blocking collectives  34.7 us (12%)
  starting transfers between devices  17.3 us (6%)
  matrix products  16.1 us (5%)
  between operations  13.6 us (5%)
    all_gather x1, waiting for transfers between devices, local(): piece = lax.all_gather(updated, 'img', axis=0, tiled=True)  107 us
    psum x1, blocking collectives, scales(): lax.psum((jnp.sum(own_drift * own_drift, axis=(1, 2, 3, 4)), jnp.sum(tang...  34.7 us
    all_gather x1, local copies, waits for them, and re-layouts, local(): piece = lax.all_gather(updated, 'img', axis=0, tiled=True)  19.8 us
    dot_general x1, matrix products, local(): jnp.dot(table, flat, precision=lax.Precision.HIGHEST, preferred_element_t...  16.1 us
    ppermute x3, waiting for transfers between devices, with_halo(): lax.ppermute(lax.slice_in_dim(block, 0, width, axis=dim), axis, backward)  9.65 us
    ppermute x3, starting transfers between devices, with_halo(): lax.ppermute(lax.slice_in_dim(block, block.shape[dim] - width, None, axis...  9.44 us
    add x16, other arithmetic, drift(): mobile = 0.5 + 1.0 / (1.0 + phi * phi)  8.8 us
    dynamic_update_slice x16, other arithmetic, all_drifts(): return lax.map(lambda field: drift(field, face), window)  7.95 us
  transfers between devices with their start and end apart: 7, of which 4 were waited for; matrix products, arithmetic and copies ran while one was open for 7% of the time, Pallas kernels for 0%

commit v1 on v0

v1 whole, which is shorter than its diff:
```python
import functools

import jax
import jax.numpy as jnp
from jax import lax
from jax.experimental import pallas as pl
from jax.experimental.pallas import tpu as pltpu
from jax.sharding import PartitionSpec as P

WLEVELS = 16
KAPPA = 0.25
COUPLE = 0.3
STEP_SIZE = 0.004
EPSILON = 1e-06

F32 = jnp.float32
HALO = 4
GX = 4
LIMIT = 24 * 1024 * 1024


def turn(value, shift):
    return pltpu.roll(value, shift % 128, 1)


def face_open(z, total):
    return jnp.where((z >= 0) & (z + 1 < total), 1.0, 0.0).astype(F32)


def drift_kernel(total, depth, place, body, side_a, side_b, ext, mu, half, own, squares, sems):
    copies = [
        pltpu.make_async_copy(body, ext.at[:, pl.ds(HALO, depth)], sems.at[0]),
        pltpu.make_async_copy(side_a, ext.at[:, pl.ds(place[1], HALO)], sems.at[1]),
        pltpu.make_async_copy(side_b, ext.at[:, pl.ds(place[2], HALO)], sems.at[2]),
    ]
    for copy in copies:
        copy.start()
    for copy in copies:
        copy.wait()
    zero = place[0] - HALO

    def potential(e, carry):
        here = [[ext[f, e, x] for x in range(GX)] for f in range(2)]
        for f in range(2):
            for x in range(GX):
                phi = here[f][x]
                around = ext[f, e - 1, x] + ext[f, e + 1, x]
                around = around + (here[f][(x + 1) % GX] + here[f][(x - 1) % GX])
                around = around + (turn(phi, 1) + turn(phi, -1))
                square = phi * phi
                mu[f, e, x] = phi * (square + (6.0 * KAPPA - 1.0)) + COUPLE * here[1 - f][x] - KAPPA * around
                half[f, e, x] = 0.25 + 0.5 / (1.0 + square)
        return carry

    lax.fori_loop(1, depth + 2 * HALO - 1, potential, 0)

    def face_z(e, f, x):
        return (half[f, e, x] + half[f, e + 1, x]) * (mu[f, e + 1, x] - mu[f, e, x])

    def flux(e, carry):
        lower, acc = carry
        is_open = face_open(zero + e, total)
        counted = jnp.where((e >= HALO) & (e < depth + HALO), 1.0, 0.0).astype(F32)
        upper = []
        for f in range(2):
            m = [mu[f, e, x] for x in range(GX)]
            h = [half[f, e, x] for x in range(GX)]
            side = [(h[x] + h[(x + 1) % GX]) * (m[(x + 1) % GX] - m[x]) for x in range(GX)]
            for x in range(GX):
                along = (h[x] + turn(h[x], -1)) * (turn(m[x], -1) - m[x])
                up = face_z(e, f, x) * is_open
                value = (side[x] - side[(x - 1) % GX]) + (along - turn(along, 1)) + (up - lower[f * GX + x])
                own[f, e, x] = value
                acc = acc + value * value * counted
                upper.append(up)
        return tuple(upper), acc

    first = face_open(zero + 1, total)
    lower = tuple(face_z(1, f, x) * first for f in range(2) for x in range(GX))
    _, acc = lax.fori_loop(2, depth + 2 * HALO - 2, flux, (lower, jnp.zeros((8, 128), F32)))
    squares[...] = acc


def neighbours(ext, before, after, e, f, x, rows):
    index = (f * rows + (e - 2)) * GX + x
    here = ext[f, e, x]
    sub = lax.broadcasted_iota(jnp.int32, (8, 128), 0)
    prev = jnp.where(sub == 0, before[pl.ds(index, 1), :], pltpu.roll(here, 1, 0))
    following = jnp.where(sub == 7, after[pl.ds(index, 1), :], pltpu.roll(here, 7, 0))
    return here, prev, following


def sums_kernel(depth, ext, before, after, squares, sums):
    def step(e, acc):
        for f in range(2):
            for x in range(GX):
                _, prev, following = neighbours(ext, before, after, e, f, x, depth + 4)
                d = following - prev
                acc = acc + d * d
        return acc

    acc = lax.fori_loop(HALO, depth + HALO, step, jnp.zeros((8, 128), F32))
    sub = lax.broadcasted_iota(jnp.int32, (8, 128), 0)
    lane = lax.broadcasted_iota(jnp.int32, (8, 128), 1)
    drift_sq = jnp.sum(squares[...], axis=1, keepdims=True)
    tangent_sq = jnp.sum(acc, axis=1, keepdims=True)
    row = jnp.where(lane == sub, drift_sq, jnp.where(lane == sub + 8, tangent_sq, 0.0))
    sums[...] = jnp.broadcast_to(jnp.sum(row, axis=0, keepdims=True), sums.shape)


def update_kernel(total, depth, images, place, ext, before, after, mu, half, own, sums, weight, out, m_ref, bar, inner):
    zero = place[0] - HALO
    sub = lax.broadcasted_iota(jnp.int32, (8, 128), 0)
    lane = lax.broadcasted_iota(jnp.int32, (8, 128), 1)
    added = jnp.sum(sums[...], axis=0, keepdims=True)
    drift_sq = jnp.sum(jnp.where(lane == sub, added, 0.0), axis=1, keepdims=True)
    tangent_sq = jnp.sum(jnp.where(lane == sub + 8, added, 0.0), axis=1, keepdims=True)
    rate = (images - 1) / 2.0
    scale = jnp.sqrt(drift_sq) / jnp.sqrt(tangent_sq * (rate * rate) + EPSILON)
    by_tangent = jnp.broadcast_to(scale * rate, (8, 128))
    by_second = jnp.broadcast_to(scale * scale * float((images - 1) ** 2), (8, 128))
    index = place[3] + sub
    step_size = jnp.where((index > 0) & (index < images - 1), STEP_SIZE, 0.0).astype(F32)

    def momentum(e, carry):
        for f in range(2):
            for x in range(GX):
                _, prev, following = neighbours(ext, before, after, e, f, x, depth + 4)
                m_ref[f, e, x] = by_tangent * (following - prev) - own[f, e, x]
        return carry

    lax.fori_loop(2, depth + 2 * HALO - 2, momentum, 0)

    def face_z(e, f, x, is_open):
        dm = m_ref[f, e + 1, x] - m_ref[f, e, x]
        dmu = mu[f, e + 1, x] - mu[f, e, x]
        g = (half[f, e, x] + half[f, e + 1, x]) * dm * is_open
        return g, dm * dmu * is_open

    def adjoint(e, carry):
        is_open = face_open(zero + e, total)
        inside = jnp.where((zero + e >= 0) & (zero + e < total), 1.0, 0.0).astype(F32)
        upper = []
        for f in range(2):
            m = [m_ref[f, e, x] for x in range(GX)]
            p = [mu[f, e, x] for x in range(GX)]
            h = [half[f, e, x] for x in range(GX)]
            side = []
            for x in range(GX):
                n = (x + 1) % GX
                dm = m[n] - m[x]
                side.append(((h[x] + h[n]) * dm, dm * (p[n] - p[x])))
            for x in range(GX):
                dm = turn(m[x], -1) - m[x]
                g_y = (h[x] + turn(h[x], -1)) * dm
                q_y = dm * (turn(p[x], -1) - p[x])
                g_z, q_z = face_z(e, f, x, is_open)
                g_low, q_low = carry[f * GX + x]
                b = (x - 1) % GX
                g = (side[x][0] - side[b][0]) + (g_y - turn(g_y, 1)) + (g_z - g_low)
                q = (side[x][1] + side[b][1]) + (q_y + turn(q_y, 1)) + (q_z + q_low)
                bar[f, e, x] = g * inside
                inner[f, e, x] = q
                upper.append((g_z, q_z))
        return tuple(upper)

    first = face_open(zero + 2, total)
    lax.fori_loop(
        3,
        depth + 2 * HALO - 3,
        adjoint,
        tuple(face_z(2, f, x, first) for f in range(2) for x in range(GX)),
    )

    def finish(r, carry):
        for zz in range(2):
            e = 2 * r + zz + HALO
            for f in range(2):
                g = [bar[f, e, x] for x in range(GX)]
                for x in range(GX):
                    phi, prev, following = neighbours(ext, before, after, e, f, x, depth + 4)
                    around = bar[f, e - 1, x] + bar[f, e + 1, x]
                    around = around + (g[(x + 1) % GX] + g[(x - 1) % GX])
                    around = around + (turn(g[x], 1) + turn(g[x], -1))
                    inverse = 2.0 * half[f, e, x] - 0.5
                    pulled = phi * (inverse * inverse) * inner[f, e, x]
                    pulled = pulled + (3.0 * (phi * phi) + (6.0 * KAPPA - 1.0)) * g[x]
                    pulled = pulled + COUPLE * bar[1 - f, e, x] - KAPPA * around
                    second = (following - phi) + (prev - phi)
                    out[r, f * 2 * GX + zz * GX + x] = phi + step_size * (by_second * second + pulled)
        out[r, 4 * GX] = weight[...]
        return carry

    lax.fori_loop(0, depth // 2, finish, 0)


def mix_kernel(images, rows, sources, got, out):
    block = (rows + 1) * 8

    def step(j, carry):
        first, other = sources[j, 0], sources[j, 1]
        a = (first // 8) * block + first % 8
        b = (other // 8) * block + other % 8
        w = got[pl.ds((j // 8) * block + rows * 8 + j % 8, 1), :]
        for part in range(rows // 8):
            one = got[pl.ds(a + part * 64, 8, stride=8), :]
            two = got[pl.ds(b + part * 64, 8, stride=8), :]
            out[pl.ds(pl.multiple_of(j * rows + part * 8, 8), 8), :] = w * one + (1.0 - w) * two
        return carry

    lax.fori_loop(0, images, step, 0)


ANY = pl.BlockSpec(memory_space=pl.ANY)
VMEM = pl.BlockSpec(memory_space=pltpu.VMEM)
SMEM = pl.BlockSpec(memory_space=pltpu.SMEM)


def call(kernel, ins, in_specs, outs, scratch=(), flops=0, moved=0):
    return pl.pallas_call(
        kernel,
        in_specs=in_specs,
        out_specs=jax.tree.map(lambda _: VMEM, outs),
        out_shape=outs,
        scratch_shapes=list(scratch),
        compiler_params=pltpu.CompilerParams(vmem_limit_bytes=LIMIT),
        cost_estimate=pl.CostEstimate(flops=flops, bytes_accessed=moved, transcendentals=0),
    )(*ins)


def swaps(count):
    near = [(i, i ^ 1) for i in range(count)]
    far = [pair for i in range(1, count - 1, 2) for pair in ((i, i + 1), (i + 1, i))]
    return near, far


def local(state, sources, weight_index):
    img_count, slab_count = lax.axis_size("img"), lax.axis_size("slab")
    img_rank, slab_rank = lax.axis_index("img"), lax.axis_index("slab")
    per_dev, _, depth, _, _ = state.shape
    images, total = per_dev * img_count, depth * slab_count
    even_img, even_slab = img_rank % 2 == 0, slab_rank % 2 == 0

    body = state.transpose(1, 2, 3, 0, 4)
    top, bottom = body[:, -HALO:], body[:, :HALO]
    near, far = swaps(slab_count)
    side_a = lax.ppermute(jnp.where(even_slab, top, bottom), "slab", near)
    side_b = lax.ppermute(jnp.where(even_slab, bottom, top), "slab", far)

    low = jnp.where(even_slab, side_b, side_a)[:, 2:]
    high = jnp.where(even_slab, side_a, side_b)[:, :2]
    ends = [
        jnp.concatenate([low[:, :, :, i], body[:, :, :, i], high[:, :, :, i]], axis=1).reshape(-1, 128)
        for i in (0, per_dev - 1)
    ]
    near, far = swaps(img_count)
    image_a = lax.ppermute(jnp.where(even_img, ends[1], ends[0]), "img", near)
    image_b = lax.ppermute(jnp.where(even_img, ends[0], ends[1]), "img", far)
    before = jnp.where(even_img, image_b, image_a)
    after = jnp.where(even_img, image_a, image_b)

    place = jnp.stack(
        [
            slab_rank * depth,
            jnp.where(even_slab, depth + HALO, 0),
            jnp.where(even_slab, 0, depth + HALO),
            img_rank * per_dev,
        ]
    ).astype(jnp.int32)
    wide = jax.ShapeDtypeStruct((2, depth + 2 * HALO, GX, 8, 128), F32)
    tile = jax.ShapeDtypeStruct((8, 128), F32)
    ext, mu, half, own, squares = call(
        functools.partial(drift_kernel, total, depth),
        (place, body, side_a, side_b),
        [SMEM, ANY, ANY, ANY],
        [wide, wide, wide, wide, tile],
        [pltpu.SemaphoreType.DMA((3,))],
        flops=20_000_000,
        moved=8_000_000,
    )
    sums = call(
        functools.partial(sums_kernel, depth),
        (ext, before, after, squares),
        [VMEM] * 4,
        jax.ShapeDtypeStruct((slab_count, 128), F32),
    )
    sums = lax.all_to_all(sums, "slab", 0, 0, tiled=True)
    weight = jnp.broadcast_to(((weight_index.astype(F32) + 1.0) / (WLEVELS + 1.0))[:, None], (8, 128))
    rows = 4 * GX
    updated = call(
        functools.partial(update_kernel, total, depth, images),
        (place, ext, before, after, mu, half, own, sums, weight),
        [SMEM] + [VMEM] * 8,
        jax.ShapeDtypeStruct((depth // 2, rows + 1, 8, 128), F32),
        [pltpu.VMEM(wide.shape, F32)] * 3,
    )
    got = lax.all_to_all(updated, "img", 0, 0, tiled=True)
    new = call(
        functools.partial(mix_kernel, images, rows),
        (sources, got.reshape(-1, 128)),
        [SMEM, VMEM],
        jax.ShapeDtypeStruct((images * rows, 128), F32),
    )
    new = lax.all_to_all(new.reshape(img_count, per_dev, 2, 2, GX, 128), "img", 0, 0, tiled=True)
    return new.transpose(1, 2, 0, 3, 4, 5).reshape(state.shape)


def solution(mesh):
    return jax.shard_map(
        local,
        mesh=mesh,
        in_specs=(P("img", None, "slab", None, None), P(), P("img")),
        out_specs=P("img", None, "slab", None, None),
        check_vma=False,
    )
```

time: 295 us -> 113 us (0.38)
  waiting for transfers between devices: 119 us -> 26.7 us
  local copies, waits for them, and re-layouts: 51.6 us -> 10.6 us
  other arithmetic: 39.7 us -> 0.22 us
  Pallas kernels: 0 us -> 25.4 us
  matrix products: 16.1 us -> 0 us
  blocking collectives: 34.7 us -> 18.8 us
  starting transfers between devices: 17.3 us -> 31.1 us
  between operations: 13.6 us -> 0.17 us
    all_gather x1 -> x0, waiting for transfers between devices: 107 us -> none  [local(): piece = lax.all_gather(updated, 'img', axis=0, tiled=True)]
    psum x1 -> x0, blocking collectives: 34.7 us -> none  [scales(): lax.psum((jnp.sum(own_drift * own_drift, axis=(1, 2, 3, 4)), jnp.sum(tang...]
    pallas_call x0 -> x4, Pallas kernels: none -> 25.4 us  [call(): pl.pallas_call(kernel, in_specs=in_specs, out_specs=jax.tree.map(lambda _...]
    all_to_all x0 -> x2, waiting for transfers between devices: none -> 25.2 us  [the longest x1 16.4 us: local(): got = lax.all_to_all(updated, 'img', 0, 0, tiled=True)]
    all_to_all x0 -> x2, starting transfers between devices: none -> 21.4 us  [the longest x1 15.2 us: local(): sums = lax.all_to_all(sums, 'slab', 0, 0, tiled=True)]
    all_gather x1 -> x0, local copies, waits for them, and re-layouts: 19.8 us -> none  [local(): piece = lax.all_gather(updated, 'img', axis=0, tiled=True)]
    all_to_all x0 -> x1, blocking collectives: none -> 18.8 us  [local(): lax.all_to_all(new.reshape(img_count, per_dev, 2, 2, GX, 128), 'img', 0,...]
    slice x179 -> x2, local copies, waits for them, and re-layouts: 16.5 us -> 0.18 us  [the longest x1 0.16 us: local(): body[:, :, :, i]]
  transfers between devices with their start and end apart: 7 -> 6, of which waited for: 4 -> 3; matrix products, arithmetic and copies ran while one was open for 7% -> 0% of each run, Pallas kernels for 0% -> 9%
where the time goes in v1:
time: 113 us
  starting transfers between devices  31.1 us (28%)
  waiting for transfers between devices  26.7 us (24%)
  Pallas kernels  25.4 us (22%)
  blocking collectives  18.8 us (17%)
  local copies, waits for them, and re-layouts  10.6 us (9%)
    pallas_call x4, Pallas kernels, call(): pl.pallas_call(kernel, in_specs=in_specs, out_specs=jax.tree.map(lambda _...  25.4 us
    all_to_all x1, blocking collectives, local(): lax.all_to_all(new.reshape(img_count, per_dev, 2, 2, GX, 128), 'img', 0,...  18.8 us
    all_to_all x1, waiting for transfers between devices, local(): got = lax.all_to_all(updated, 'img', 0, 0, tiled=True)  16.4 us
    all_to_all x1, starting transfers between devices, local(): sums = lax.all_to_all(sums, 'slab', 0, 0, tiled=True)  15.2 us
    unnamed x18, local copies, waits for them, and re-layouts  9.09 us
    all_to_all x1, waiting for transfers between devices, local(): sums = lax.all_to_all(sums, 'slab', 0, 0, tiled=True)  8.76 us
    all_to_all x1, starting transfers between devices, local(): got = lax.all_to_all(updated, 'img', 0, 0, tiled=True)  6.17 us
    ppermute x1, starting transfers between devices, local(): image_b = lax.ppermute(jnp.where(even_img, ends[0], ends[1]), 'img', far)  5.15 us
  transfers between devices with their start and end apart: 6, of which 3 were waited for; matrix products, arithmetic and copies ran while one was open for 0% of the time, Pallas kernels for 9%

profile of v1, /device:TPU:1, one launch (start us, length us, event | category | flops | bytes accessed | tf_op | source)
XLA Modules:
  0.0 113.0 jit_solution(611166925985929991)
XLA Ops:
  0.0 1.8 %copy.15 = f32[8,2,32,4,128]{4,0,3,2,1:T(8,128)S(1)} copy(f32[8,2,32,4,128]{4,3,2,1,0:T(4,128)} %param.3) | data formatting | bytes 2097152 | tf_op args[0]
  1.9 3.8 %collective-permute-start = (f32[2,4,4,8,128]{4,3,2,1,0:T(8,128)S(1)}, f32[2,4,4,8,128]{4,3,2,1,0:T(8,128)S(1)}, u32[]{:S(2)}, u32[]{:S(2)}) collective-permute-start(f32[2,4,4,8,128]{4,3,2,1,0:T(8,128)S(1)} %get-tuple-element.18), channel_id=1, source_target_pairs={{0,1},{1,0},{2,3},{3,2},{4,5},{5,4},{6,7},{7,6},{8,9},{9,8},{10,11... | collective-permute-start | bytes 393224 | tf_op jit(solution)/shard_map/ppermute | solution.py:247
  5.7 0.7 collective-permute-start.1
  6.4 0.2 fusion
  6.5 1.5 %collective-permute-done.side_a = f32[2,4,4,8,128]{4,3,2,1,0:T(8,128)S(1)} collective-permute-done((f32[2,4,4,8,128]{4,3,2,1,0:T(8,128)S(1)}, f32[2,4,4,8,128]{4,3,2,1,0:T(8,128)S(1)}, u32[]{:S(2)}, u32[]{:S(2)}) %collective-permute-start) | collective-permute-done | bytes 131104 | tf_op jit(solution)/shard_map/ppermute | solution.py:247
  8.1 0.0 collective-permute-done.1.side_b
  8.1 0.1 broadcast_select_fusion
  8.2 5.1 %collective-permute-start.2 = (f32[288,128]{1,0:T(8,128)S(1)}, f32[288,128]{1,0:T(8,128)S(1)}, u32[]{:S(2)}, u32[]{:S(2)}) collective-permute-start(f32[288,128]{1,0:T(8,128)S(1)} %bitcast.35), channel_id=1, source_target_pairs={{16,32},{32,16},{48,64},{64,48},{80,96},{96,80},{112,128},{128,112... | collective-permute-start | bytes 442376 | tf_op jit(solution)/shard_map/ppermute | solution.py:258
  13.3 0.1 collective-permute-start.3
  13.5 0.1 pad_add_fusion.place
  13.5 9.9 %shard_map.37 = (f32[2,40,4,8,128]{4,3,2,1,0:T(8,128)S(1)}, f32[2,40,4,8,128]{4,3,2,1,0:T(8,128)S(1)}, f32[2,40,4,8,128]{4,3,2,1,0:T(8,128)S(1)}, f32[2,40,4,8,128]{4,3,2,1,0:T(8,128)S(1)}, f32[8,128]{1,0:T(8,128)S(1)}) custom-call(s32[4]{0:T(128)S(1)} %pad_add_fusion.place, f32[2,32,4,8,128]{4,3,2,1,0:T(8,128)S(1)} %bitcast.27, ...), custom_call_target="tpu_custom_call" | custom-call | flops 20000000 | bytes 8000000 | tf_op jit(solution)/shard_map/pallas_call | solution.py:220
  23.4 0.0 copy-start
  23.4 1.1 copy-done
  24.5 1.1 copy-done.2
  25.5 1.1 copy-done.4
  26.6 0.0 collective-permute-done.2
  26.6 0.0 collective-permute-done.3
  26.7 1.2 %shard_map.38 = f32[16,128]{1,0:T(8,128)} custom-call(f32[2,40,4,8,128]{4,3,2,1,0:T(8,128)S(1)} %get-tuple-element.10.ext, f32[288,128]{1,0:T(8,128)S(1)} %get-tuple-element.20.before, f32[288,128]{1,0:T(8,128)S(1)} %get-tuple-element.19.after, f32[8,128]{1,0:T(8,128)S(1)} %get-tuple-element.14.squares), custom_call_target="tpu_custom_call" | custom-call | tf_op jit(solution)/shard_map/pallas_call | solution.py:220
  27.8 15.2 %all-to-all-start = ((f32[16,1,128]{2,1,0:T(1,128)}), f32[16,1,128]{2,1,0:T(1,128)S(1)}, u32[]{:S(2)}, u32[]{:S(2)}) async-start(f32[16,1,128]{2,1,0:T(1,128)} %bitcast.14), calls=%async_computation | async-start | bytes 16384 | tf_op jit(solution)/shard_map/all_to_all | solution.py:287
  43.0 0.0 copy-done.7
  43.0 8.8 %all-to-all-done = f32[16,1,128]{2,1,0:T(1,128)S(1)} async-done(((f32[16,1,128]{2,1,0:T(1,128)}), f32[16,1,128]{2,1,0:T(1,128)S(1)}, u32[]{:S(2)}, u32[]{:S(2)}) %all-to-all-start) | async-done | bytes 8224 | tf_op jit(solution)/shard_map/all_to_all | solution.py:287
  51.8 0.1 broadcast_in_dim.2.weight
  51.9 1.3 %copy-done.1 = f32[2,40,4,8,128]{4,3,2,1,0:T(8,128)S(1)} copy-done((f32[2,40,4,8,128]{4,3,2,1,0:T(8,128)S(1)}, f32[2,40,4,8,128]{4,3,2,1,0:T(8,128)}, u32[]{:S(2)}) %copy-start.1) | copy-done | bytes 1310744
  53.2 1.3 %copy-done.3 = f32[2,40,4,8,128]{4,3,2,1,0:T(8,128)S(1)} copy-done((f32[2,40,4,8,128]{4,3,2,1,0:T(8,128)S(1)}, f32[2,40,4,8,128]{4,3,2,1,0:T(8,128)}, u32[]{:S(2)}) %copy-start.3) | copy-done | bytes 1310744
  54.5 1.3 %copy-done.5 = f32[2,40,4,8,128]{4,3,2,1,0:T(8,128)S(1)} copy-done((f32[2,40,4,8,128]{4,3,2,1,0:T(8,128)S(1)}, f32[2,40,4,8,128]{4,3,2,1,0:T(8,128)}, u32[]{:S(2)}) %copy-start.5) | copy-done | bytes 1310744
  55.8 9.6 %shard_map.39 = f32[16,17,8,128]{3,2,1,0:T(8,128)} custom-call(s32[4]{0:T(128)S(1)} %pad_add_fusion.place, f32[2,40,4,8,128]{4,3,2,1,0:T(8,128)S(1)} %get-tuple-element.10.ext, f32[288,128]{1,0:T(8,128)S(1)} %get-tuple-element.20.before, f32[288,128]{1,0:T(8,128)S(1)} %get-tuple-element.19.after, f32[2,40,4,8,128]{4,3,2,1,0:T(8,128)S(1)} %copy-done.1, ...), custom_call_target="tpu_custom_call" | custom-call | tf_op jit(solution)/shard_map/pallas_call | solution.py:220
  65.4 6.2 %all-to-all-start.1 = ((f32[16,17,8,128]{3,2,1,0:T(8,128)}), f32[16,17,8,128]{3,2,1,0:T(8,128)S(1)}, u32[]{:S(2)}, u32[]{:S(2)}) async-start(f32[16,17,8,128]{3,2,1,0:T(8,128)} %shard_map.39), calls=%async_computation.1 | async-start | bytes 2228224 | tf_op jit(solution)/shard_map/all_to_all | solution.py:297
  71.6 0.1 copy.11.sources
  71.7 16.4 %all-to-all-done.1 = f32[16,17,8,128]{3,2,1,0:T(8,128)S(1)} async-done(((f32[16,17,8,128]{3,2,1,0:T(8,128)}), f32[16,17,8,128]{3,2,1,0:T(8,128)S(1)}, u32[]{:S(2)}, u32[]{:S(2)}) %all-to-all-start.1) | async-done | bytes 1114144 | tf_op jit(solution)/shard_map/all_to_all | solution.py:297
  88.1 4.8 %shard_map.40 = f32[2048,128]{1,0:T(8,128)S(1)} custom-call(s32[128,2]{1,0:T(8,128)S(1)} %copy.11.sources, f32[2176,128]{1,0:T(8,128)S(1)} %bitcast.28), custom_call_target="tpu_custom_call" | custom-call | tf_op jit(solution)/shard_map/pallas_call | solution.py:220
  93.0 18.8 %all_to_all.21 = f32[16,8,2,2,4,128]{5,4,3,2,1,0:T(4,128)S(1)} all-to-all(f32[16,8,2,2,4,128]{5,4,3,2,1,0:T(4,128)S(1)} %bitcast.29), channel_id=1, replica_groups=mesh['img'=16,'slab'=16] {'img'}, dimensions={0} | all-to-all | bytes 2097152 | tf_op jit(solution)/shard_map/all_to_all | solution.py:304
  111.8 1.2 %copy.12 = f32[8,2,16,2,4,128]{5,4,3,2,1,0:T(4,128)} copy(f32[8,2,16,2,4,128]{5,4,3,1,0,2:T(4,128)S(1)} %bitcast.31) | data formatting | bytes 2097152 | tf_op jit(solution)/shard_map/transpose | solution.py:305
  (13 shorter events, 0.1 us)
Async XLA Ops:
  1.9 6.2 %collective-permute-start = (f32[2,4,4,8,128]{4,3,2,1,0:T(8,128)S(1)}, f32[2,4,4,8,128]{4,3,2,1,0:T(8,128)S(1)}, u32[]{:S(2)}, u32[]{:S(2)}) collective-permute-start(f32[2,4,4,8,128]{4,3,2,1,0:T(8,128)S(1)} %get-tuple-element.18), channel_id=1, source_target_pairs={{0,1},{1,0},{2,3},{3,2},{4,5},{5,4},{6,7},{7,6},{8,9},{9,8},{10,11... | collective-permute-start | bytes 393224 | tf_op jit(solution)/shard_map/ppermute | solution.py:247
  5.7 2.4 %collective-permute-start.1 = (f32[2,4,4,8,128]{4,3,2,1,0:T(8,128)S(1)}, f32[2,4,4,8,128]{4,3,2,1,0:T(8,128)S(1)}, u32[]{:S(2)}, u32[]{:S(2)}) collective-permute-start(f32[2,4,4,8,128]{4,3,2,1,0:T(8,128)S(1)} %get-tuple-element.17), channel_id=1, source_target_pairs={{1,2},{2,1},{3,4},{4,3},{5,6},{6,5},{7,8},{8,7},{9,10},{10,9},{11,... | collective-permute-start | bytes 393224 | tf_op jit(solution)/shard_map/ppermute | solution.py:248
  8.2 18.4 %collective-permute-start.2 = (f32[288,128]{1,0:T(8,128)S(1)}, f32[288,128]{1,0:T(8,128)S(1)}, u32[]{:S(2)}, u32[]{:S(2)}) collective-permute-start(f32[288,128]{1,0:T(8,128)S(1)} %bitcast.35), channel_id=1, source_target_pairs={{16,32},{32,16},{48,64},{64,48},{80,96},{96,80},{112,128},{128,112... | collective-permute-start | bytes 442376 | tf_op jit(solution)/shard_map/ppermute | solution.py:258
  13.3 13.3 %collective-permute-start.3 = (f32[288,128]{1,0:T(8,128)S(1)}, f32[288,128]{1,0:T(8,128)S(1)}, u32[]{:S(2)}, u32[]{:S(2)}) collective-permute-start(f32[288,128]{1,0:T(8,128)S(1)} %bitcast.34), channel_id=1, source_target_pairs={{0,16},{16,0},{32,48},{48,32},{64,80},{80,64},{96,112},{112,96},{1... | collective-permute-start | bytes 442376 | tf_op jit(solution)/shard_map/ppermute | solution.py:257
  23.4 1.1 copy-start
  24.5 1.1 copy-start.2
  25.5 1.1 copy-start.4
  26.6 16.4 %copy-start.7 = (s32[8]{0:T(128)S(1)}, s32[8]{0:T(128)}, u32[]{:S(2)}) copy-start(s32[8]{0:T(128)} %param.5) | copy-start | bytes 100
  27.8 24.0 %all-to-all-start = ((f32[16,1,128]{2,1,0:T(1,128)}), f32[16,1,128]{2,1,0:T(1,128)S(1)}, u32[]{:S(2)}, u32[]{:S(2)}) async-start(f32[16,1,128]{2,1,0:T(1,128)} %bitcast.14), calls=%async_computation | async-start | bytes 16384 | tf_op jit(solution)/shard_map/all_to_all | solution.py:287
  51.9 1.3 %copy-start.1 = (f32[2,40,4,8,128]{4,3,2,1,0:T(8,128)S(1)}, f32[2,40,4,8,128]{4,3,2,1,0:T(8,128)}, u32[]{:S(2)}) copy-start(f32[2,40,4,8,128]{4,3,2,1,0:T(8,128)} %copy-done) | copy-start | bytes 3932164
  53.2 1.3 %copy-start.3 = (f32[2,40,4,8,128]{4,3,2,1,0:T(8,128)S(1)}, f32[2,40,4,8,128]{4,3,2,1,0:T(8,128)}, u32[]{:S(2)}) copy-start(f32[2,40,4,8,128]{4,3,2,1,0:T(8,128)} %copy-done.2) | copy-start | bytes 3932164
  54.5 1.3 %copy-start.5 = (f32[2,40,4,8,128]{4,3,2,1,0:T(8,128)S(1)}, f32[2,40,4,8,128]{4,3,2,1,0:T(8,128)}, u32[]{:S(2)}) copy-start(f32[2,40,4,8,128]{4,3,2,1,0:T(8,128)} %copy-done.4) | copy-start | bytes 3932164
  65.4 6.2 %copy-start.6 = (s32[128,2]{0,1:T(2,128)S(1)}, s32[128,2]{0,1:T(2,128)}, u32[]{:S(2)}) copy-start(s32[128,2]{0,1:T(2,128)} %param.4) | copy-start | bytes 3076
  65.4 22.7 %all-to-all-start.1 = ((f32[16,17,8,128]{3,2,1,0:T(8,128)}), f32[16,17,8,128]{3,2,1,0:T(8,128)S(1)}, u32[]{:S(2)}, u32[]{:S(2)}) async-start(f32[16,17,8,128]{3,2,1,0:T(8,128)} %shard_map.39), calls=%async_computation.1 | async-start | bytes 2228224 | tf_op jit(solution)/shard_map/all_to_all | solution.py:297

commit v2 on v1

--- a/solution.py
+++ b/solution.py
@@ -16,11 +16,18 @@
 F32 = jnp.float32
 HALO = 4
 GX = 4
-LIMIT = 24 * 1024 * 1024
+LIMIT = 8 * 1024 * 1024
+U1, U2, U3, U4, U5, U6, U7 = 2, 4, 4, 4, 2, 1, 8
 
 
 def turn(value, shift):
     return pltpu.roll(value, shift % 128, 1)
+
+
+def recip(d):
+    r = pltpu.reciprocal(d, approx=True)
+    r = r * (2.0 - d * r)
+    return r * (2.0 - d * r)
 
 
 def face_open(z, total):
@@ -49,10 +56,10 @@
                 around = around + (turn(phi, 1) + turn(phi, -1))
                 square = phi * phi
                 mu[f, e, x] = phi * (square + (6.0 * KAPPA - 1.0)) + COUPLE * here[1 - f][x] - KAPPA * around
-                half[f, e, x] = 0.25 + 0.5 / (1.0 + square)
+                half[f, e, x] = 0.25 + 0.5 * recip(1.0 + square)
         return carry
 
-    lax.fori_loop(1, depth + 2 * HALO - 1, potential, 0)
+    lax.fori_loop(1, depth + 2 * HALO - 1, potential, 0, unroll=U1)
 
     def face_z(e, f, x):
         return (half[f, e, x] + half[f, e + 1, x]) * (mu[f, e + 1, x] - mu[f, e, x])
@@ -77,7 +84,7 @@
 
     first = face_open(zero + 1, total)
     lower = tuple(face_z(1, f, x) * first for f in range(2) for x in range(GX))
-    _, acc = lax.fori_loop(2, depth + 2 * HALO - 2, flux, (lower, jnp.zeros((8, 128), F32)))
+    _, acc = lax.fori_loop(2, depth + 2 * HALO - 2, flux, (lower, jnp.zeros((8, 128), F32)), unroll=U2)
     squares[...] = acc
 
 
@@ -99,7 +106,7 @@
                 acc = acc + d * d
         return acc
 
-    acc = lax.fori_loop(HALO, depth + HALO, step, jnp.zeros((8, 128), F32))
+    acc = lax.fori_loop(HALO, depth + HALO, step, jnp.zeros((8, 128), F32), unroll=U3)
     sub = lax.broadcasted_iota(jnp.int32, (8, 128), 0)
     lane = lax.broadcasted_iota(jnp.int32, (8, 128), 1)
     drift_sq = jnp.sum(squares[...], axis=1, keepdims=True)
@@ -129,7 +136,7 @@
                 m_ref[f, e, x] = by_tangent * (following - prev) - own[f, e, x]
         return carry
 
-    lax.fori_loop(2, depth + 2 * HALO - 2, momentum, 0)
+    lax.fori_loop(2, depth + 2 * HALO - 2, momentum, 0, unroll=U4)
 
     def face_z(e, f, x, is_open):
         dm = m_ref[f, e + 1, x] - m_ref[f, e, x]
@@ -170,6 +177,7 @@
         depth + 2 * HALO - 3,
         adjoint,
         tuple(face_z(2, f, x, first) for f in range(2) for x in range(GX)),
+        unroll=U5,
     )
 
     def finish(r, carry):
@@ -187,28 +195,26 @@
                     pulled = pulled + (3.0 * (phi * phi) + (6.0 * KAPPA - 1.0)) * g[x]
                     pulled = pulled + COUPLE * bar[1 - f, e, x] - KAPPA * around
                     second = (following - phi) + (prev - phi)
-                    out[r, f * 2 * GX + zz * GX + x] = phi + step_size * (by_second * second + pulled)
-        out[r, 4 * GX] = weight[...]
+                    out[r, pl.ds(f * 2 * GX + zz * GX + x, 8, stride=4 * GX), :] = phi + step_size * (by_second * second + pulled)
+        out[r, pl.ds(32 * GX, 8), :] = weight[...]
         return carry
 
-    lax.fori_loop(0, depth // 2, finish, 0)
-
-
-def mix_kernel(images, rows, sources, got, out):
+    lax.fori_loop(0, depth // 2, finish, 0, unroll=U6)
+
+
+def mix_kernel(images, rows, starts, got, out):
     block = (rows + 1) * 8
 
     def step(j, carry):
-        first, other = sources[j, 0], sources[j, 1]
-        a = (first // 8) * block + first % 8
-        b = (other // 8) * block + other % 8
+        a = pl.multiple_of(starts[j], 8)
+        b = pl.multiple_of(starts[images + j], 8)
         w = got[pl.ds((j // 8) * block + rows * 8 + j % 8, 1), :]
-        for part in range(rows // 8):
-            one = got[pl.ds(a + part * 64, 8, stride=8), :]
-            two = got[pl.ds(b + part * 64, 8, stride=8), :]
-            out[pl.ds(pl.multiple_of(j * rows + part * 8, 8), 8), :] = w * one + (1.0 - w) * two
+        for part in range(0, rows, 8):
+            one, two = got[pl.ds(a + part, 8), :], got[pl.ds(b + part, 8), :]
+            out[pl.ds(pl.multiple_of(j * rows + part, 8), 8), :] = w * one + (1.0 - w) * two
         return carry
 
-    lax.fori_loop(0, images, step, 0)
+    lax.fori_loop(0, images, step, 0, unroll=U7)
 
 
 ANY = pl.BlockSpec(memory_space=pl.ANY)
@@ -241,8 +247,9 @@
     images, total = per_dev * img_count, depth * slab_count
     even_img, even_slab = img_rank % 2 == 0, slab_rank % 2 == 0
 
-    body = state.transpose(1, 2, 3, 0, 4)
-    top, bottom = body[:, -HALO:], body[:, :HALO]
+    top = state[:, :, -HALO:].transpose(1, 2, 3, 0, 4)
+    bottom = state[:, :, :HALO].transpose(1, 2, 3, 0, 4)
+    body = lax.optimization_barrier(state).transpose(1, 2, 3, 0, 4)
     near, far = swaps(slab_count)
     side_a = lax.ppermute(jnp.where(even_slab, top, bottom), "slab", near)
     side_b = lax.ppermute(jnp.where(even_slab, bottom, top), "slab", far)
@@ -291,13 +298,14 @@
         functools.partial(update_kernel, total, depth, images),
         (place, ext, before, after, mu, half, own, sums, weight),
         [SMEM] + [VMEM] * 8,
-        jax.ShapeDtypeStruct((depth // 2, rows + 1, 8, 128), F32),
+        jax.ShapeDtypeStruct((depth // 2, (rows + 1) * 8, 128), F32),
         [pltpu.VMEM(wide.shape, F32)] * 3,
     )
     got = lax.all_to_all(updated, "img", 0, 0, tiled=True)
+    starts = (sources // per_dev) * ((rows + 1) * 8) + (sources % per_dev) * rows
     new = call(
         functools.partial(mix_kernel, images, rows),
-        (sources, got.reshape(-1, 128)),
+        (starts.T.reshape(-1), got.reshape(-1, 128)),
         [SMEM, VMEM],
         jax.ShapeDtypeStruct((images * rows, 128), F32),
     )

time: 113 us -> 102 us (0.903)
  Pallas kernels: 25.4 us -> 14.5 us
    pallas_call x4, Pallas kernels: 25.4 us -> 14.5 us  [call(): pl.pallas_call(kernel, in_specs=in_specs, out_specs=jax.tree.map(lambda _...]
    ppermute x1, starting transfers between devices: 0.09 us -> 3.7 us  [local(): image_a = lax.ppermute(jnp.where(even_img, ends[1], ends[0]), 'img', near)]
    ppermute x1, starting transfers between devices: 5.15 us -> 1.91 us  [local(): image_b = lax.ppermute(jnp.where(even_img, ends[0], ends[1]), 'img', far)]
    unnamed x18, local copies, waits for them, and re-layouts: 9.09 us -> 7.14 us
  transfers between devices with their start and end apart: 6 -> 6, of which waited for: 3 -> 3; matrix products, arithmetic and copies ran while one was open for 0% -> 1% of each run, Pallas kernels for 9% -> 5%
where the time goes in v2:
time: 102 us; the launch traced here: 101 us
  starting transfers between devices  31 us (30%)
  waiting for transfers between devices  26.2 us (26%)
  blocking collectives  18.8 us (18%)
  Pallas kernels  14.5 us (14%)
  local copies, waits for them, and re-layouts  10.3 us (10%)
    all_to_all x1, blocking collectives, local(): lax.all_to_all(new.reshape(img_count, per_dev, 2, 2, GX, 128), 'img', 0,...  18.8 us
    all_to_all x1, waiting for transfers between devices, local(): got = lax.all_to_all(updated, 'img', 0, 0, tiled=True)  16.5 us
    all_to_all x1, starting transfers between devices, local(): sums = lax.all_to_all(sums, 'slab', 0, 0, tiled=True)  14.8 us
    pallas_call x4, Pallas kernels, call(): pl.pallas_call(kernel, in_specs=in_specs, out_specs=jax.tree.map(lambda _...  14.5 us
    all_to_all x1, waiting for transfers between devices, local(): sums = lax.all_to_all(sums, 'slab', 0, 0, tiled=True)  8.76 us
    unnamed x18, local copies, waits for them, and re-layouts  7.14 us
    all_to_all x1, starting transfers between devices, local(): got = lax.all_to_all(updated, 'img', 0, 0, tiled=True)  6.06 us
    ppermute x1, starting transfers between devices, local(): side_a = lax.ppermute(jnp.where(even_slab, top, bottom), 'slab', near)  3.83 us
  transfers between devices with their start and end apart: 6, of which 3 were waited for; matrix products, arithmetic and copies ran while one was open for 1% of the time, Pallas kernels for 5%

profile of v2, /device:TPU:1, one launch (start us, length us, event | category | flops | bytes accessed | tf_op | source)
XLA Modules:
  0.0 101.3 jit_solution(16443555502687678809)
XLA Ops:
  0.0 1.1 %fusion.4 = (f32[8,2,4,4,128]{4,3,2,1,0:T(4,128)S(1)}, f32[8,2,4,4,128]{4,3,2,1,0:T(4,128)S(1)}) fusion(f32[8,2,32,4,128]{4,3,2,1,0:T(4,128)} %param.3), kind=kLoop, calls=%fused_computation.22 | loop fusion | bytes 524288 | tf_op jit(solution)/shard_map/slice | solution.py:250
  1.1 0.2 select_bitcast_fusion
  1.2 3.8 %collective-permute-start = (f32[2,4,4,8,128]{4,3,2,1,0:T(8,128)S(1)}, f32[2,4,4,8,128]{4,3,2,1,0:T(8,128)S(1)}, u32[]{:S(2)}, u32[]{:S(2)}) collective-permute-start(f32[2,4,4,8,128]{4,3,2,1,0:T(8,128)S(1)} %get-tuple-element.26), channel_id=1, source_target_pairs={{0,1},{1,0},{2,3},{3,2},{4,5},{5,4},{6,7},{7,6},{8,9},{9,8},{10,11... | collective-permute-start | bytes 393224 | tf_op jit(solution)/shard_map/ppermute | solution.py:254
  5.1 0.7 collective-permute-start.1
  5.8 0.6 copy.23
  6.4 0.2 fusion.3
  6.6 0.9 collective-permute-done.side_a
  7.4 0.0 collective-permute-done.1.side_b
  7.5 0.1 broadcast_select_fusion
  7.6 3.7 %collective-permute-start.3 = (f32[288,128]{1,0:T(8,128)S(1)}, f32[288,128]{1,0:T(8,128)S(1)}, u32[]{:S(2)}, u32[]{:S(2)}) collective-permute-start(f32[288,128]{1,0:T(8,128)S(1)} %bitcast.42), channel_id=1, source_target_pairs={{0,16},{16,0},{32,48},{48,32},{64,80},{80,64},{96,112},{112,96},{1... | collective-permute-start | bytes 442376 | tf_op jit(solution)/shard_map/ppermute | solution.py:264
  11.3 1.9 %collective-permute-start.2 = (f32[288,128]{1,0:T(8,128)S(1)}, f32[288,128]{1,0:T(8,128)S(1)}, u32[]{:S(2)}, u32[]{:S(2)}) collective-permute-start(f32[288,128]{1,0:T(8,128)S(1)} %bitcast.41), channel_id=1, source_target_pairs={{16,32},{32,16},{48,64},{64,48},{80,96},{96,80},{112,128},{128,112... | collective-permute-start | bytes 442376 | tf_op jit(solution)/shard_map/ppermute | solution.py:265
  13.2 0.1 pad_add_fusion.place
  13.3 4.7 %shard_map.37 = (f32[2,40,4,8,128]{4,3,2,1,0:T(8,128)S(1)}, f32[2,40,4,8,128]{4,3,2,1,0:T(8,128)S(1)}, f32[2,40,4,8,128]{4,3,2,1,0:T(8,128)S(1)}, f32[2,40,4,8,128]{4,3,2,1,0:T(8,128)S(1)}, f32[8,128]{1,0:T(8,128)S(1)}) custom-call(s32[4]{0:T(128)S(1)} %pad_add_fusion.place, f32[2,32,4,8,128]{4,3,2,1,0:T(8,128)S(1)} %bitcast.34, ...), custom_call_target="tpu_custom_call" | custom-call | flops 20000000 | bytes 8000000 | tf_op jit(solution)/shard_map/pallas_call | solution.py:226
  18.0 1.1 %copy-done = f32[2,40,4,8,128]{4,3,2,1,0:T(8,128)} copy-done((f32[2,40,4,8,128]{4,3,2,1,0:T(8,128)}, f32[2,40,4,8,128]{4,3,2,1,0:T(8,128)S(1)}, u32[]{:S(2)}) %copy-start) | copy-done | bytes 1310744
  19.1 1.1 %copy-done.2 = f32[2,40,4,8,128]{4,3,2,1,0:T(8,128)} copy-done((f32[2,40,4,8,128]{4,3,2,1,0:T(8,128)}, f32[2,40,4,8,128]{4,3,2,1,0:T(8,128)S(1)}, u32[]{:S(2)}) %copy-start.2) | copy-done | bytes 1310744
  20.1 1.1 %copy-done.4 = f32[2,40,4,8,128]{4,3,2,1,0:T(8,128)} copy-done((f32[2,40,4,8,128]{4,3,2,1,0:T(8,128)}, f32[2,40,4,8,128]{4,3,2,1,0:T(8,128)S(1)}, u32[]{:S(2)}) %copy-start.4) | copy-done | bytes 1310744
  21.2 0.0 collective-permute-done.3
  21.2 0.0 collective-permute-done.2
  21.2 1.0 %shard_map.38 = f32[16,128]{1,0:T(8,128)} custom-call(f32[2,40,4,8,128]{4,3,2,1,0:T(8,128)S(1)} %get-tuple-element.10.ext, f32[288,128]{1,0:T(8,128)S(1)} %get-tuple-element.20.before, f32[288,128]{1,0:T(8,128)S(1)} %get-tuple-element.19.after, f32[8,128]{1,0:T(8,128)S(1)} %get-tuple-element.14.squares), custom_call_target="tpu_custom_call" | custom-call | tf_op jit(solution)/shard_map/pallas_call | solution.py:226
  22.3 14.8 %all-to-all-start = ((f32[16,1,128]{2,1,0:T(1,128)}), f32[16,1,128]{2,1,0:T(1,128)S(1)}, u32[]{:S(2)}, u32[]{:S(2)}) async-start(f32[16,1,128]{2,1,0:T(1,128)} %bitcast.18), calls=%async_computation | async-start | bytes 16384 | tf_op jit(solution)/shard_map/all_to_all | solution.py:294
  37.1 0.0 copy-done.8
  37.1 8.8 %all-to-all-done = f32[16,1,128]{2,1,0:T(1,128)S(1)} async-done(((f32[16,1,128]{2,1,0:T(1,128)}), f32[16,1,128]{2,1,0:T(1,128)S(1)}, u32[]{:S(2)}, u32[]{:S(2)}) %all-to-all-start) | async-done | bytes 8224 | tf_op jit(solution)/shard_map/all_to_all | solution.py:294
  45.9 0.1 broadcast_in_dim.2.weight
  46.0 1.3 %copy-done.1 = f32[2,40,4,8,128]{4,3,2,1,0:T(8,128)S(1)} copy-done((f32[2,40,4,8,128]{4,3,2,1,0:T(8,128)S(1)}, f32[2,40,4,8,128]{4,3,2,1,0:T(8,128)}, u32[]{:S(2)}) %copy-start.1) | copy-done | bytes 1310744
  47.3 1.3 %copy-done.3 = f32[2,40,4,8,128]{4,3,2,1,0:T(8,128)S(1)} copy-done((f32[2,40,4,8,128]{4,3,2,1,0:T(8,128)S(1)}, f32[2,40,4,8,128]{4,3,2,1,0:T(8,128)}, u32[]{:S(2)}) %copy-start.3) | copy-done | bytes 1310744
  48.6 1.3 %copy-done.5 = f32[2,40,4,8,128]{4,3,2,1,0:T(8,128)S(1)} copy-done((f32[2,40,4,8,128]{4,3,2,1,0:T(8,128)S(1)}, f32[2,40,4,8,128]{4,3,2,1,0:T(8,128)}, u32[]{:S(2)}) %copy-start.5) | copy-done | bytes 1310744
  49.9 7.2 %shard_map.39 = f32[16,136,128]{2,1,0:T(8,128)} custom-call(s32[4]{0:T(128)S(1)} %pad_add_fusion.place, f32[2,40,4,8,128]{4,3,2,1,0:T(8,128)S(1)} %get-tuple-element.10.ext, f32[288,128]{1,0:T(8,128)S(1)} %get-tuple-element.20.before, f32[288,128]{1,0:T(8,128)S(1)} %get-tuple-element.19.after, f32[2,40,4,8,128]{4,3,2,1,0:T(8,128)S(1)} %copy-done.1, ...), custom_call_target="tpu_custom_call" | custom-call | tf_op jit(solution)/shard_map/pallas_call | solution.py:226
  57.1 6.1 %all-to-all-start.1 = ((f32[16,136,128]{2,1,0:T(8,128)}), f32[16,136,128]{2,1,0:T(8,128)S(1)}, u32[]{:S(2)}, u32[]{:S(2)}) async-start(f32[16,136,128]{2,1,0:T(8,128)} %shard_map.39), calls=%async_computation.1 | async-start | bytes 2228224 | tf_op jit(solution)/shard_map/all_to_all | solution.py:304
  63.2 16.5 %all-to-all-done.1 = f32[16,136,128]{2,1,0:T(8,128)S(1)} async-done(((f32[16,136,128]{2,1,0:T(8,128)}), f32[16,136,128]{2,1,0:T(8,128)S(1)}, u32[]{:S(2)}, u32[]{:S(2)}) %all-to-all-start.1) | async-done | bytes 1114144 | tf_op jit(solution)/shard_map/all_to_all | solution.py:304
  79.7 1.6 %shard_map.40 = f32[2048,128]{1,0:T(8,128)S(1)} custom-call(s32[256]{0:T(256)S(1)} %fusion.2.starts, f32[2176,128]{1,0:T(8,128)S(1)} %bitcast.35), custom_call_target="tpu_custom_call" | custom-call | tf_op jit(solution)/shard_map/pallas_call | solution.py:226
  81.3 18.8 %all_to_all.21 = f32[16,8,2,2,4,128]{5,4,3,2,1,0:T(4,128)S(1)} all-to-all(f32[16,8,2,2,4,128]{5,4,3,2,1,0:T(4,128)S(1)} %bitcast.36), channel_id=1, replica_groups=mesh['img'=16,'slab'=16] {'img'}, dimensions={0} | all-to-all | bytes 2097152 | tf_op jit(solution)/shard_map/all_to_all | solution.py:312
  100.1 1.2 %copy.14 = f32[8,2,16,2,4,128]{5,4,3,2,1,0:T(4,128)} copy(f32[8,2,16,2,4,128]{5,4,3,1,0,2:T(4,128)S(1)} %bitcast.38) | data formatting | bytes 2097152 | tf_op jit(solution)/shard_map/transpose | solution.py:313
  (16 shorter events, 0.1 us)
Async XLA Ops:
  0.0 5.7 %copy-start.6 = (f32[8,2,32,4,128]{4,3,2,1,0:T(4,128)S(1)}, f32[8,2,32,4,128]{4,3,2,1,0:T(4,128)}, u32[]{:S(2)}) copy-start(f32[8,2,32,4,128]{4,3,2,1,0:T(4,128)} %param.3) | copy-start | bytes 3145732
  1.2 6.2 %collective-permute-start = (f32[2,4,4,8,128]{4,3,2,1,0:T(8,128)S(1)}, f32[2,4,4,8,128]{4,3,2,1,0:T(8,128)S(1)}, u32[]{:S(2)}, u32[]{:S(2)}) collective-permute-start(f32[2,4,4,8,128]{4,3,2,1,0:T(8,128)S(1)} %get-tuple-element.26), channel_id=1, source_target_pairs={{0,1},{1,0},{2,3},{3,2},{4,5},{5,4},{6,7},{7,6},{8,9},{9,8},{10,11... | collective-permute-start | bytes 393224 | tf_op jit(solution)/shard_map/ppermute | solution.py:254
  5.1 2.4 %collective-permute-start.1 = (f32[2,4,4,8,128]{4,3,2,1,0:T(8,128)S(1)}, f32[2,4,4,8,128]{4,3,2,1,0:T(8,128)S(1)}, u32[]{:S(2)}, u32[]{:S(2)}) collective-permute-start(f32[2,4,4,8,128]{4,3,2,1,0:T(8,128)S(1)} %get-tuple-element.25), channel_id=1, source_target_pairs={{1,2},{2,1},{3,4},{4,3},{5,6},{6,5},{7,8},{8,7},{9,10},{10,9},{11,... | collective-permute-start | bytes 393224 | tf_op jit(solution)/shard_map/ppermute | solution.py:255
  7.6 13.6 %collective-permute-start.3 = (f32[288,128]{1,0:T(8,128)S(1)}, f32[288,128]{1,0:T(8,128)S(1)}, u32[]{:S(2)}, u32[]{:S(2)}) collective-permute-start(f32[288,128]{1,0:T(8,128)S(1)} %bitcast.42), channel_id=1, source_target_pairs={{0,16},{16,0},{32,48},{48,32},{64,80},{80,64},{96,112},{112,96},{1... | collective-permute-start | bytes 442376 | tf_op jit(solution)/shard_map/ppermute | solution.py:264
  11.3 9.9 %collective-permute-start.2 = (f32[288,128]{1,0:T(8,128)S(1)}, f32[288,128]{1,0:T(8,128)S(1)}, u32[]{:S(2)}, u32[]{:S(2)}) collective-permute-start(f32[288,128]{1,0:T(8,128)S(1)} %bitcast.41), channel_id=1, source_target_pairs={{16,32},{32,16},{48,64},{64,48},{80,96},{96,80},{112,128},{128,112... | collective-permute-start | bytes 442376 | tf_op jit(solution)/shard_map/ppermute | solution.py:265
  18.0 1.1 %copy-start = (f32[2,40,4,8,128]{4,3,2,1,0:T(8,128)}, f32[2,40,4,8,128]{4,3,2,1,0:T(8,128)S(1)}, u32[]{:S(2)}) copy-start(f32[2,40,4,8,128]{4,3,2,1,0:T(8,128)S(1)} %get-tuple-element.11.mu) | copy-start | bytes 3932164
  19.1 1.1 %copy-start.2 = (f32[2,40,4,8,128]{4,3,2,1,0:T(8,128)}, f32[2,40,4,8,128]{4,3,2,1,0:T(8,128)S(1)}, u32[]{:S(2)}) copy-start(f32[2,40,4,8,128]{4,3,2,1,0:T(8,128)S(1)} %get-tuple-element.12.half) | copy-start | bytes 3932164
  20.1 1.1 %copy-start.4 = (f32[2,40,4,8,128]{4,3,2,1,0:T(8,128)}, f32[2,40,4,8,128]{4,3,2,1,0:T(8,128)S(1)}, u32[]{:S(2)}) copy-start(f32[2,40,4,8,128]{4,3,2,1,0:T(8,128)S(1)} %get-tuple-element.13.own) | copy-start | bytes 3932164
  21.2 15.9 %copy-start.8 = (s32[8]{0:T(128)S(1)}, s32[8]{0:T(128)}, u32[]{:S(2)}) copy-start(s32[8]{0:T(128)} %param.5) | copy-start | bytes 100
  22.3 23.6 %all-to-all-start = ((f32[16,1,128]{2,1,0:T(1,128)}), f32[16,1,128]{2,1,0:T(1,128)S(1)}, u32[]{:S(2)}, u32[]{:S(2)}) async-start(f32[16,1,128]{2,1,0:T(1,128)} %bitcast.18), calls=%async_computation | async-start | bytes 16384 | tf_op jit(solution)/shard_map/all_to_all | solution.py:294
  46.0 1.3 %copy-start.1 = (f32[2,40,4,8,128]{4,3,2,1,0:T(8,128)S(1)}, f32[2,40,4,8,128]{4,3,2,1,0:T(8,128)}, u32[]{:S(2)}) copy-start(f32[2,40,4,8,128]{4,3,2,1,0:T(8,128)} %copy-done) | copy-start | bytes 3932164
  47.3 1.3 %copy-start.3 = (f32[2,40,4,8,128]{4,3,2,1,0:T(8,128)S(1)}, f32[2,40,4,8,128]{4,3,2,1,0:T(8,128)}, u32[]{:S(2)}) copy-start(f32[2,40,4,8,128]{4,3,2,1,0:T(8,128)} %copy-done.2) | copy-start | bytes 3932164
  48.6 1.3 %copy-start.5 = (f32[2,40,4,8,128]{4,3,2,1,0:T(8,128)S(1)}, f32[2,40,4,8,128]{4,3,2,1,0:T(8,128)}, u32[]{:S(2)}) copy-start(f32[2,40,4,8,128]{4,3,2,1,0:T(8,128)} %copy-done.4) | copy-start | bytes 3932164
  57.1 6.1 %copy-start.7 = (s32[128,2]{0,1:T(2,128)S(1)}, s32[128,2]{0,1:T(2,128)}, u32[]{:S(2)}) copy-start(s32[128,2]{0,1:T(2,128)} %param.4) | copy-start | bytes 3076
  57.1 22.6 %all-to-all-start.1 = ((f32[16,136,128]{2,1,0:T(8,128)}), f32[16,136,128]{2,1,0:T(8,128)S(1)}, u32[]{:S(2)}, u32[]{:S(2)}) async-start(f32[16,136,128]{2,1,0:T(8,128)} %shard_map.39), calls=%async_computation.1 | async-start | bytes 2228224 | tf_op jit(solution)/shard_map/all_to_all | solution.py:304

commit v3 on v2

v3 whole, which is shorter than its diff:
```python
import functools

import jax
import jax.numpy as jnp
from jax import lax
from jax.experimental import pallas as pl
from jax.experimental.pallas import tpu as pltpu
from jax.sharding import PartitionSpec as P

WLEVELS = 16
KAPPA = 0.25
COUPLE = 0.3
STEP_SIZE = 0.004
EPSILON = 1e-06

F32 = jnp.float32
GX = 4
LIMIT = 14 * 1024 * 1024
MOST = 121 * 512 * 1024
UNROLL = 2


def turn(value, shift):
    return pltpu.roll(value, shift % 128, 1)


def recip(d):
    r = pltpu.reciprocal(d, approx=True)
    r = r * (2.0 - d * r)
    return r * (2.0 - d * r)


def load(ref, z):
    return [[ref[f, z, x] for x in range(GX)] for f in range(2)]


def store(ref, z, layer):
    for f in range(2):
        for x in range(GX):
            ref[f, z, x] = layer[f][x]


def each(fn, *layers):
    return [[fn(*(layer[f][x] for layer in layers)) for x in range(GX)] for f in range(2)]


def potential(below, here, above):
    mu, half = [], []
    for f in range(2):
        mu.append([])
        half.append([])
        for x in range(GX):
            phi = here[f][x]
            around = below[f][x] + above[f][x]
            around = around + (here[f][(x + 1) % GX] + here[f][(x - 1) % GX])
            around = around + (turn(phi, 1) + turn(phi, -1))
            square = phi * phi
            mu[f].append(phi * (square + (6.0 * KAPPA - 1.0)) + COUPLE * here[1 - f][x] - KAPPA * around)
            half[f].append(0.25 + 0.5 * recip(1.0 + square))
    return mu, half


def face(mu, half, mu_up, half_up):
    return each(lambda p, h, q, k: (h + k) * (q - p), mu, half, mu_up, half_up)


def outflow(mu, half, lower, upper):
    layer = []
    for f in range(2):
        p, h = mu[f], half[f]
        side = [(h[x] + h[(x + 1) % GX]) * (p[(x + 1) % GX] - p[x]) for x in range(GX)]
        along = [(h[x] + turn(h[x], -1)) * (turn(p[x], -1) - p[x]) for x in range(GX)]
        layer.append(
            [
                (side[x] - side[x - 1]) + (along[x] - turn(along[x], 1)) + (upper[f][x] - lower[f][x])
                for x in range(GX)
            ]
        )
    return layer


def drift_kernel(depth, body, fields):
    mu, half, own, kept = (fields.at[i] for i in range(4))
    for z in (0, depth - 1):
        store(kept, z, load(body, z))

    def first_fields(z, carry):
        here = load(body, z)
        store(kept, z, here)
        p, h = potential(load(body, z - 1), here, load(body, z + 1))
        store(mu, z, p)
        store(half, z, h)
        return carry

    lax.fori_loop(1, depth - 1, first_fields, 0, unroll=2)

    def flux(z, lower):
        p, h = load(mu, z), load(half, z)
        upper = face(p, h, load(mu, z + 1), load(half, z + 1))
        store(own, z, outflow(p, h, lower, upper))
        return upper

    first = face(load(mu, 1), load(half, 1), load(mu, 2), load(half, 2))
    lax.fori_loop(2, depth - 2, flux, first, unroll=4)


def rim(depth, phi, known, low_open, high_open, reach):
    fields = {}
    for z in [*range(-reach, 1), *range(depth - 1, depth + reach)]:
        fields[z] = potential(phi(z - 1), phi(z), phi(z + 1))
    for z in (1, 2, depth - 3, depth - 2):
        fields[z] = known(z)
    faces, drifts = {}, {}
    for z in [*range(-reach, 2), *range(depth - 3, depth + reach - 1)]:
        faces[z] = face(*fields[z], *fields[z + 1])
    faces[-1] = each(lambda v: v * low_open, faces[-1])
    faces[depth - 1] = each(lambda v: v * high_open, faces[depth - 1])
    for z in [*range(1 - reach, 2), *range(depth - 2, depth + reach - 1)]:
        drifts[z] = outflow(*fields[z], faces[z - 1], faces[z])
    return fields, drifts


def ends_open():
    rank = lax.axis_index("slab")
    low = jnp.where(rank > 0, 1.0, 0.0).astype(F32)
    high = jnp.where(rank < lax.axis_size("slab") - 1, 1.0, 0.0).astype(F32)
    return low, high


def even(axis):
    return 1 - lax.axis_index(axis) % 2


def neighbours(here, before, after, f, z, x, rows):
    index = (f * rows + (z + 2)) * GX + x
    sub = lax.broadcasted_iota(jnp.int32, (8, 128), 0)
    prev = jnp.where(sub == 0, before[pl.ds(index, 1), :], pltpu.roll(here, 1, 0))
    following = jnp.where(sub == 7, after[pl.ds(index, 1), :], pltpu.roll(here, 7, 0))
    return prev, following


def fetch(pairs, sems):
    copies = [pltpu.make_async_copy(source, target, sems.at[i]) for i, (source, target) in enumerate(pairs)]
    for copy in copies:
        copy.start()

    def wait():
        for copy in copies:
            copy.wait()

    return wait


def arrivals(side_a, side_b, image_a, image_b, side, image, sems):
    slab, img = even("slab"), even("img")
    return fetch(
        [
            (side_a, side.at[slab]),
            (side_b, side.at[1 - slab]),
            (image_a, image.at[img]),
            (image_b, image.at[1 - img]),
        ],
        sems,
    )


def layer_of(depth, body, side):
    def phi(z):
        return load(side.at[0], z + 4) if z < 0 else load(side.at[1], z - depth) if z >= depth else load(body, z)

    return phi


def sums_kernel(depth, side_a, side_b, image_a, image_b, fields, sums, side, image, sems):
    arrived = arrivals(side_a, side_b, image_a, image_b, side, image, sems)
    mu, half, own, body = (fields.at[i] for i in range(4))

    def squares(z, kept):
        one, two = jnp.zeros((8, 128), F32), jnp.zeros((8, 128), F32)
        for x in range(GX):
            one = one + own[0, z, x] * own[0, z, x]
            two = two + own[1, z, x] * own[1, z, x]
        return kept + (one + two)

    kept = lax.fori_loop(2, depth - 2, squares, jnp.zeros((8, 128), F32), unroll=4)
    arrived()
    _, drifts = rim(depth, layer_of(depth, body, side), lambda z: (load(mu, z), load(half, z)), *ends_open(), 1)
    for z in (0, 1, depth - 2, depth - 1):
        for f in range(2):
            for x in range(GX):
                kept = kept + drifts[z][f][x] * drifts[z][f][x]

    def step(z, acc):
        for f in range(2):
            for x in range(GX):
                prev, following = neighbours(body[f, z, x], image.at[0], image.at[1], f, z, x, depth + 4)
                d = following - prev
                acc = acc + d * d
        return acc

    acc = lax.fori_loop(0, depth, step, jnp.zeros((8, 128), F32), unroll=4)
    sub = lax.broadcasted_iota(jnp.int32, (8, 128), 0)
    lane = lax.broadcasted_iota(jnp.int32, (8, 128), 1)
    drift_sq = jnp.sum(kept, axis=1, keepdims=True)
    tangent_sq = jnp.sum(acc, axis=1, keepdims=True)
    row = jnp.where(lane == sub, drift_sq, jnp.where(lane == sub + 8, tangent_sq, 0.0))
    sums[...] = jnp.broadcast_to(jnp.sum(row, axis=0, keepdims=True), sums.shape)


def rim_layers(depth):
    fields = (-2, -1, 0, depth - 1, depth, depth + 1)
    drifts = (-2, -1, 0, 1, depth - 2, depth - 1, depth, depth + 1)
    return {z: i for i, z in enumerate(fields)}, {z: i for i, z in enumerate(drifts)}


def prepare_kernel(depth, side_a, side_b, image_a, image_b, fields, diff, both, rim_mu, rim_half, rim_own, *scratch):
    side, image, sems, body, ends, more = scratch
    arrived = arrivals(side_a, side_b, image_a, image_b, side, image, sems)
    pairs = [(fields.at[3], body)]
    for i in range(2):
        pairs.append((fields.at[i, :, pl.ds(1, 2)], ends.at[i, :, pl.ds(0, 2)]))
        pairs.append((fields.at[i, :, pl.ds(depth - 3, 2)], ends.at[i, :, pl.ds(2, 2)]))
    fetch(pairs, more)()
    arrived()
    place = {1: 0, 2: 1, depth - 3: 2, depth - 2: 3}
    phi = layer_of(depth, body, side)
    known, drifts = rim(depth, phi, lambda z: (load(ends.at[0], place[z]), load(ends.at[1], place[z])), *ends_open(), 3)
    slot, drift_slot = rim_layers(depth)
    for z, i in slot.items():
        store(rim_mu, i, known[z][0])
        store(rim_half, i, known[z][1])
    for z, i in drift_slot.items():
        store(rim_own, i, drifts[z])

    def images(z, here):
        for f in range(2):
            for x in range(GX):
                prev, following = neighbours(here[f][x], image.at[0], image.at[1], f, z, x, depth + 4)
                diff[f, z + 2, x] = following - prev
                both[f, z + 2, x] = following + prev

    for z in (-2, -1, depth, depth + 1):
        images(z, phi(z))

    def inside(z, carry):
        images(z, load(body, z))
        return carry

    lax.fori_loop(0, depth, inside, 0, unroll=4)


def update_kernel(depth, images, given, diff_given, both_given, rim_mu_given, rim_half_given, rim_own_given, *refs):
    sums, level, out, m_ref, bar, inner, fields, diff, both, rim_mu, rim_half, rim_own, sems = refs
    cut = depth // 4
    parts = [(2, cut), (cut, depth - 2)]
    rim_here = fetch(
        [
            (rim_own_given, rim_own),
            (diff_given.at[:, pl.ds(0, 4)], diff.at[:, pl.ds(0, 4)]),
            (diff_given.at[:, pl.ds(depth, 4)], diff.at[:, pl.ds(depth, 4)]),
        ],
        sems.at[0],
    )
    parts_here = []
    for i, (low, high) in enumerate(parts):
        own_part, diff_part = pl.ds(low, high - low), pl.ds(low + 2, high - low)
        parts_here.append(
            fetch(
                [
                    (given.at[2, :, own_part], fields.at[2, :, own_part]),
                    (diff_given.at[:, diff_part], diff.at[:, diff_part]),
                ],
                sems.at[1 + i],
            )
        )
    flux_here = fetch(
        [
            (rim_mu_given, rim_mu),
            (rim_half_given, rim_half),
            (given.at[0], fields.at[0]),
            (given.at[1], fields.at[1]),
        ],
        sems.at[3],
    )
    rest_here = fetch([(given.at[3], fields.at[3]), (both_given, both)], sems.at[4])
    mu, half, own, body = (fields.at[i] for i in range(4))
    slot, drift_slot = rim_layers(depth)
    sub = lax.broadcasted_iota(jnp.int32, (8, 128), 0)
    lane = lax.broadcasted_iota(jnp.int32, (8, 128), 1)
    added = jnp.sum(sums[...], axis=0, keepdims=True)
    drift_sq = jnp.sum(jnp.where(lane == sub, added, 0.0), axis=1, keepdims=True)
    tangent_sq = jnp.sum(jnp.where(lane == sub + 8, added, 0.0), axis=1, keepdims=True)
    rate = (images - 1) / 2.0
    scale = jnp.sqrt(drift_sq) / jnp.sqrt(tangent_sq * (rate * rate) + EPSILON)
    by_tangent = jnp.broadcast_to(scale * rate, (8, 128))
    by_second = jnp.broadcast_to(scale * scale * float((images - 1) ** 2), (8, 128))
    index = lax.axis_index("img") * 8 + sub
    step_size = jnp.where((index > 0) & (index < images - 1), STEP_SIZE, 0.0).astype(F32)
    low_open, high_open = ends_open()
    weight = jnp.zeros((8, 128), F32)
    for i in range(8):
        weight = jnp.where(sub == i, level[i].astype(F32), weight)
    weight = (weight + 1.0) / (WLEVELS + 1.0)

    def momentum(z, drift):
        store(m_ref, z + 2, each(lambda d, b: by_tangent * d - b, load(diff, z + 2), drift))

    rim_here()
    for z, i in drift_slot.items():
        momentum(z, load(rim_own, i))

    def inside(z, carry):
        momentum(z, load(own, z))
        return carry

    for (first, last), here in zip(parts, parts_here):
        here()
        lax.fori_loop(first, last, inside, 0, unroll=2)
    flux_here()

    def known(z):
        if isinstance(z, int) and z in slot:
            return load(rim_mu, slot[z]), load(rim_half, slot[z])
        return load(mu, z), load(half, z)

    def pair(z, up):
        (p, h), (q, k) = known(z), known(up)
        m, n = load(m_ref, z + 2), load(m_ref, up + 2)
        g = each(lambda a, b, c, d: (a + b) * (d - c), h, k, m, n)
        return g, each(lambda a, b, c, d: (b - a) * (d - c), p, q, m, n)

    def adjoint(z, lower, upper, is_open=None):
        p, h = known(z)
        m = load(m_ref, z + 2)
        for f in range(2):
            side = []
            for x in range(GX):
                n = (x + 1) % GX
                dm = m[f][n] - m[f][x]
                side.append(((h[f][x] + h[f][n]) * dm, dm * (p[f][n] - p[f][x])))
            for x in range(GX):
                dm = turn(m[f][x], -1) - m[f][x]
                g_y = (h[f][x] + turn(h[f][x], -1)) * dm
                q_y = dm * (turn(p[f][x], -1) - p[f][x])
                g = (side[x][0] - side[x - 1][0]) + (g_y - turn(g_y, 1)) + (upper[0][f][x] - lower[0][f][x])
                q = (side[x][1] + side[x - 1][1]) + (q_y + turn(q_y, 1)) + (upper[1][f][x] + lower[1][f][x])
                bar[f, z + 1, x] = g if is_open is None else g * is_open
                inner[f, z + 1, x] = q

    def shut(faces, is_open):
        return tuple(each(lambda v: v * is_open, layer) for layer in faces)

    faces = pair(-2, -1)
    upper = shut(pair(-1, 0), low_open)
    adjoint(-1, faces, upper, low_open)
    faces, upper = upper, pair(0, 1)
    adjoint(0, faces, upper)

    def within(z, lower):
        upper = pair(z, z + 1)
        adjoint(z, lower, upper)
        return upper

    faces = lax.fori_loop(1, depth - 2, within, upper, unroll=2)
    upper = pair(depth - 2, depth - 1)
    adjoint(depth - 2, faces, upper)
    faces, upper = upper, shut(pair(depth - 1, depth), high_open)
    adjoint(depth - 1, faces, upper)
    adjoint(depth, upper, pair(depth, depth + 1), high_open)

    def finish(r, carry):
        for zz in range(2):
            z = 2 * r + zz
            _, h = known(z)
            for f in range(2):
                g = [bar[f, z + 1, x] for x in range(GX)]
                for x in range(GX):
                    phi = body[f, z, x]
                    around = bar[f, z, x] + bar[f, z + 2, x]
                    around = around + (g[(x + 1) % GX] + g[(x - 1) % GX])
                    around = around + (turn(g[x], 1) + turn(g[x], -1))
                    inverse = 2.0 * h[f][x] - 0.5
                    pulled = phi * (inverse * inverse) * inner[f, z + 1, x]
                    pulled = pulled + (3.0 * (phi * phi) + (6.0 * KAPPA - 1.0)) * g[x]
                    pulled = pulled + COUPLE * bar[1 - f, z + 1, x] - KAPPA * around
                    second = both[f, z + 2, x] - 2.0 * phi
                    new = phi + step_size * (by_second * second + pulled)
                    out[r, pl.ds((f * 2 + zz) * GX + x, 8, stride=4 * GX), :] = new
        out[r, pl.ds(32 * GX, 8), :] = weight
        return carry

    rest_here()
    finish(0, 0)
    lax.fori_loop(1, depth // 2 - 1, finish, 0, unroll=UNROLL)
    finish(depth // 2 - 1, 0)


def mix_kernel(images, rows, starts, got, out):
    block = (rows + 1) * 8

    def step(j, carry):
        a = pl.multiple_of(starts[j], 8)
        b = pl.multiple_of(starts[images + j], 8)
        w = got[pl.ds((j // 8) * block + rows * 8 + j % 8, 1), :]
        for part in range(0, rows, 8):
            one, two = got[pl.ds(a + part, 8), :], got[pl.ds(b + part, 8), :]
            out[pl.ds(pl.multiple_of(j * rows + part, 8), 8), :] = w * one + (1.0 - w) * two
        return carry

    lax.fori_loop(0, images, step, 0, unroll=8)


ANY = pl.BlockSpec(memory_space=pl.ANY)
VMEM = pl.BlockSpec(memory_space=pltpu.VMEM)
SMEM = pl.BlockSpec(memory_space=pltpu.SMEM)


def call(kernel, ins, in_specs, outs, scratch=(), flops=0, moved=0, limit=LIMIT):
    return pl.pallas_call(
        kernel,
        in_specs=in_specs,
        out_specs=jax.tree.map(lambda _: VMEM, outs),
        out_shape=outs,
        scratch_shapes=list(scratch),
        compiler_params=pltpu.CompilerParams(vmem_limit_bytes=limit),
        cost_estimate=pl.CostEstimate(flops=flops, bytes_accessed=moved, transcendentals=0),
    )(*ins)


def swaps(count):
    near = [(i, i ^ 1) for i in range(count)]
    far = [pair for i in range(1, count - 1, 2) for pair in ((i, i + 1), (i + 1, i))]
    return near, far


def local(state, sources, weight_index):
    img_count, slab_count = lax.axis_size("img"), lax.axis_size("slab")
    img_rank, slab_rank = lax.axis_index("img"), lax.axis_index("slab")
    per_dev, _, depth, _, _ = state.shape
    images = per_dev * img_count
    even_img, even_slab = img_rank % 2 == 0, slab_rank % 2 == 0

    near, far = swaps(slab_count)

    top = state[:, :, depth - 4 :].transpose(1, 2, 3, 0, 4)
    bottom = state[:, :, :4].transpose(1, 2, 3, 0, 4)
    side_a = lax.ppermute(jnp.where(even_slab, top, bottom), "slab", near)
    side_b = lax.ppermute(jnp.where(even_slab, bottom, top), "slab", far)
    body = lax.optimization_barrier(state).transpose(1, 2, 3, 0, 4)
    fields = call(
        functools.partial(drift_kernel, depth),
        (body,),
        [VMEM],
        jax.ShapeDtypeStruct((4, *body.shape), F32),
        flops=16_000_000,
        moved=4_000_000,
    )

    low, high = jnp.where(even_slab, side_b, side_a)[:, 2:], jnp.where(even_slab, side_a, side_b)[:, :2]
    ends = [
        jnp.concatenate([low[:, :, :, i], state[i], high[:, :, :, i]], axis=1).reshape(-1, 128)
        for i in (0, per_dev - 1)
    ]
    near, far = swaps(img_count)
    image_a = lax.ppermute(jnp.where(even_img, ends[1], ends[0]), "img", near)
    image_b = lax.ppermute(jnp.where(even_img, ends[0], ends[1]), "img", far)

    def layers(count):
        return (2, count, GX, 8, 128)

    brought = [
        pltpu.VMEM((2, *layers(4)), F32),
        pltpu.VMEM((2, *image_a.shape), F32),
        pltpu.SemaphoreType.DMA((4,)),
    ]
    around = (side_a, side_b, image_a, image_b, fields)
    sums = call(
        functools.partial(sums_kernel, depth),
        around,
        [ANY] * 4 + [VMEM],
        jax.ShapeDtypeStruct((slab_count, 128), F32),
        brought,
    )
    sums = lax.all_to_all(sums, "slab", 0, 0, tiled=True)
    wide = layers(depth + 4)
    prepared = call(
        functools.partial(prepare_kernel, depth),
        around,
        [ANY] * 5,
        [jax.ShapeDtypeStruct(shape, F32) for shape in (wide, wide, layers(6), layers(6), layers(8))],
        brought
        + [pltpu.VMEM(layers(depth), F32), pltpu.VMEM((2, *layers(4)), F32), pltpu.SemaphoreType.DMA((5,))],
        flops=8_000_000,
        moved=4_000_000,
        limit=MOST,
    )
    rows = 4 * GX
    updated = call(
        functools.partial(update_kernel, depth, images),
        (fields, *prepared, sums, weight_index),
        [ANY] * 6 + [VMEM, SMEM],
        jax.ShapeDtypeStruct((depth // 2, (rows + 1) * 8, 128), F32),
        [pltpu.VMEM(wide, F32)]
        + [pltpu.VMEM(layers(depth + 2), F32)] * 2
        + [pltpu.VMEM(array.shape, F32) for array in (fields, *prepared)]
        + [pltpu.SemaphoreType.DMA((5, 4))],
        limit=MOST,
    )
    got = lax.all_to_all(updated, "img", 0, 0, tiled=True)
    starts = (sources // per_dev) * ((rows + 1) * 8) + (sources % per_dev) * rows
    new = call(
        functools.partial(mix_kernel, images, rows),
        (starts.T.reshape(-1), got.reshape(-1, 128)),
        [SMEM, VMEM],
        jax.ShapeDtypeStruct((images * rows, 128), F32),
    )
    new = lax.all_to_all(new.reshape(img_count, per_dev, 2, 2, GX, 128), "img", 0, 0, tiled=True)
    return new.transpose(1, 2, 0, 3, 4, 5).reshape(state.shape)


def solution(mesh):
    return jax.shard_map(
        local,
        mesh=mesh,
        in_specs=(P("img", None, "slab", None, None), P(), P("img")),
        out_specs=P("img", None, "slab", None, None),
        check_vma=False,
    )
```

time: 102 us -> 97.3 us (0.954)
  local copies, waits for them, and re-layouts: 10.3 us -> 3.6 us
  Pallas kernels: 14.5 us -> 20.6 us
  waiting for transfers between devices: 26.2 us -> 23.3 us
    unnamed x18 -> x16, local copies, waits for them, and re-layouts: 7.14 us -> 0.62 us
    pallas_call x4 -> x5, Pallas kernels: 14.5 us -> 20.6 us  [call(): pl.pallas_call(kernel, in_specs=in_specs, out_specs=jax.tree.map(lambda _...]
    all_to_all x1, waiting for transfers between devices: 8.76 us -> 4.36 us  [local(): sums = lax.all_to_all(sums, 'slab', 0, 0, tiled=True)]
  transfers between devices with their start and end apart: 6 -> 6, of which waited for: 3 -> 4; matrix products, arithmetic and copies ran while one was open for 1% -> 1% of each run, Pallas kernels for 5% -> 8%
where the time goes in v3:
time: 97.3 us; the launch traced here: 96.9 us
  starting transfers between devices  30.2 us (31%)
  waiting for transfers between devices  23.3 us (24%)
  Pallas kernels  20.6 us (21%)
  blocking collectives  18.8 us (19%)
  local copies, waits for them, and re-layouts  3.6 us (4%)
    pallas_call x5, Pallas kernels, call(): pl.pallas_call(kernel, in_specs=in_specs, out_specs=jax.tree.map(lambda _...  20.6 us
    all_to_all x1, blocking collectives, local(): lax.all_to_all(new.reshape(img_count, per_dev, 2, 2, GX, 128), 'img', 0,...  18.8 us
    all_to_all x1, waiting for transfers between devices, local(): got = lax.all_to_all(updated, 'img', 0, 0, tiled=True)  16.5 us
    all_to_all x1, starting transfers between devices, local(): sums = lax.all_to_all(sums, 'slab', 0, 0, tiled=True)  14.2 us
    all_to_all x1, starting transfers between devices, local(): got = lax.all_to_all(updated, 'img', 0, 0, tiled=True)  5.93 us
    all_to_all x1, waiting for transfers between devices, local(): sums = lax.all_to_all(sums, 'slab', 0, 0, tiled=True)  4.36 us
    ppermute x1, starting transfers between devices, local(): side_a = lax.ppermute(jnp.where(even_slab, top, bottom), 'slab', near)  3.83 us
    ppermute x1, starting transfers between devices, local(): image_a = lax.ppermute(jnp.where(even_img, ends[1], ends[0]), 'img', near)  3.7 us
  transfers between devices with their start and end apart: 6, of which 4 were waited for; matrix products, arithmetic and copies ran while one was open for 1% of the time, Pallas kernels for 8%

profile of v3, /device:TPU:1, one launch (start us, length us, event | category | flops | bytes accessed | tf_op | source)
XLA Modules:
  0.0 96.9 jit_solution(2259098731989056064)
XLA Ops:
  0.0 1.1 %fusion.3 = (f32[8,2,4,4,128]{4,3,2,1,0:T(4,128)S(1)}, f32[8,2,4,4,128]{4,3,2,1,0:T(4,128)S(1)}) fusion(f32[8,2,32,4,128]{4,3,2,1,0:T(4,128)} %param.3), kind=kLoop, calls=%fused_computation.19 | loop fusion | bytes 524288 | tf_op jit(solution)/shard_map/slice | solution.py:445
  1.1 0.2 select_bitcast_fusion
  1.2 3.8 %collective-permute-start = (f32[2,4,4,8,128]{4,3,2,1,0:T(8,128)S(1)}, f32[2,4,4,8,128]{4,3,2,1,0:T(8,128)S(1)}, u32[]{:S(2)}, u32[]{:S(2)}) collective-permute-start(f32[2,4,4,8,128]{4,3,2,1,0:T(8,128)S(1)} %get-tuple-element.24), channel_id=1, source_target_pairs={{0,1},{1,0},{2,3},{3,2},{4,5},{5,4},{6,7},{7,6},{8,9},{9,8},{10,11... | collective-permute-start | bytes 393224 | tf_op jit(solution)/shard_map/ppermute | solution.py:447
  5.1 0.7 collective-permute-start.1
  5.7 0.0 copy-done.5
  5.8 1.6 %collective-permute-done.side_a = f32[2,4,4,8,128]{4,3,2,1,0:T(8,128)S(1)} collective-permute-done((f32[2,4,4,8,128]{4,3,2,1,0:T(8,128)S(1)}, f32[2,4,4,8,128]{4,3,2,1,0:T(8,128)S(1)}, u32[]{:S(2)}, u32[]{:S(2)}) %collective-permute-start) | collective-permute-done | bytes 131104 | tf_op jit(solution)/shard_map/ppermute | solution.py:447
  7.4 0.0 collective-permute-done.1.side_b
  7.5 0.1 broadcast_select_fusion
  7.6 3.7 %collective-permute-start.2 = (f32[288,128]{1,0:T(8,128)S(1)}, f32[288,128]{1,0:T(8,128)S(1)}, u32[]{:S(2)}, u32[]{:S(2)}) collective-permute-start(f32[288,128]{1,0:T(8,128)S(1)} %bitcast.34), channel_id=1, source_target_pairs={{0,16},{16,0},{32,48},{48,32},{64,80},{80,64},{96,112},{112,96},{1... | collective-permute-start | bytes 442376 | tf_op jit(solution)/shard_map/ppermute | solution.py:465
  11.3 1.9 %collective-permute-start.3 = (f32[288,128]{1,0:T(8,128)S(1)}, f32[288,128]{1,0:T(8,128)S(1)}, u32[]{:S(2)}, u32[]{:S(2)}) collective-permute-start(f32[288,128]{1,0:T(8,128)S(1)} %bitcast.33), channel_id=1, source_target_pairs={{16,32},{32,16},{48,64},{64,48},{80,96},{96,80},{112,128},{128,112... | collective-permute-start | bytes 442376 | tf_op jit(solution)/shard_map/ppermute | solution.py:466
  13.2 0.6 copy.20
  13.8 3.2 %shard_map.37.fields.given = f32[4,2,32,4,8,128]{5,4,3,2,1,0:T(8,128)S(1)} custom-call(f32[2,32,4,8,128]{4,3,2,1,0:T(8,128)S(1)} %bitcast.30), custom_call_target="tpu_custom_call" | custom-call | flops 16000000 | bytes 4000000 | tf_op jit(solution)/shard_map/pallas_call | solution.py:419
  17.0 0.0 collective-permute-done.2.image_a
  17.0 0.0 copy-start.3
  17.0 0.7 collective-permute-done.3.image_b
  17.7 0.0 copy-done.1
  17.7 0.0 copy-done.2
  17.7 2.2 %shard_map.39 = f32[16,128]{1,0:T(8,128)} custom-call(f32[2,4,4,8,128]{4,3,2,1,0:T(8,128)S(1)} %collective-permute-done.side_a, f32[2,4,4,8,128]{4,3,2,1,0:T(8,128)S(1)} %collective-permute-done.1.side_b, f32[288,128]{1,0:T(8,128)S(1)} %collective-permute-done.2.image_a, f32[288,128]{1,0:T(8,128)S(1)} %collective-permute-done.3.image_b, ...), custom_call_target="tpu_custom_call" | custom-call | tf_op jit(solution)/shard_map/pallas_call | solution.py:419
  19.9 0.0 copy-done
  19.9 0.0 copy-done.3
  19.9 0.0 copy-done.4
  19.9 14.2 %all-to-all-start = ((f32[16,1,128]{2,1,0:T(1,128)}), f32[16,1,128]{2,1,0:T(1,128)S(1)}, u32[]{:S(2)}, u32[]{:S(2)}) async-start(f32[16,1,128]{2,1,0:T(1,128)} %bitcast.14), calls=%async_computation | async-start | bytes 16384 | tf_op jit(solution)/shard_map/all_to_all | solution.py:484
  34.1 4.5 %shard_map.38 = (f32[2,36,4,8,128]{4,3,2,1,0:T(8,128)}, f32[2,36,4,8,128]{4,3,2,1,0:T(8,128)}, f32[2,6,4,8,128]{4,3,2,1,0:T(8,128)}, f32[2,6,4,8,128]{4,3,2,1,0:T(8,128)}, f32[2,8,4,8,128]{4,3,2,1,0:T(8,128)}) custom-call(f32[2,4,4,8,128]{4,3,2,1,0:T(8,128)} %copy-done.1, f32[2,4,4,8,128]{4,3,2,1,0:T(8,128)} %copy-done.2, f32[288,128]{1,0:T(8,128)} %copy-done.3, ...), custom_call_target="tpu_custom_call" | custom-call | flops 8000000 | bytes 4000000 | tf_op jit(solution)/shard_map/pallas_call | solution.py:419
  38.7 4.4 %all-to-all-done = f32[16,1,128]{2,1,0:T(1,128)S(1)} async-done(((f32[16,1,128]{2,1,0:T(1,128)}), f32[16,1,128]{2,1,0:T(1,128)S(1)}, u32[]{:S(2)}, u32[]{:S(2)}) %all-to-all-start) | async-done | bytes 8224 | tf_op jit(solution)/shard_map/all_to_all | solution.py:484
  43.0 0.6 copy-done.6
  43.6 9.1 %shard_map.40 = f32[16,136,128]{2,1,0:T(8,128)} custom-call(f32[4,2,32,4,8,128]{5,4,3,2,1,0:T(8,128)} %copy-done, f32[2,36,4,8,128]{4,3,2,1,0:T(8,128)} %get-tuple-element.10.diff_given, f32[2,36,4,8,128]{4,3,2,1,0:T(8,128)} %get-tuple-element.11.both_given, f32[2,6,4,8,128]{4,3,2,1,0:T(8,128)} %get-tuple-element.12.rim_mu_given, ...), custom_call_target="tpu_custom_call" | custom-call | tf_op jit(solution)/shard_map/pallas_call | solution.py:419
  52.7 0.0 copy-start.7
  52.7 5.9 %all-to-all-start.1 = ((f32[16,136,128]{2,1,0:T(8,128)}), f32[16,136,128]{2,1,0:T(8,128)S(1)}, u32[]{:S(2)}, u32[]{:S(2)}) async-start(f32[16,136,128]{2,1,0:T(8,128)} %shard_map.40), calls=%async_computation.1 | async-start | bytes 2228224 | tf_op jit(solution)/shard_map/all_to_all | solution.py:509
  58.7 16.5 %all-to-all-done.1 = f32[16,136,128]{2,1,0:T(8,128)S(1)} async-done(((f32[16,136,128]{2,1,0:T(8,128)}), f32[16,136,128]{2,1,0:T(8,128)S(1)}, u32[]{:S(2)}, u32[]{:S(2)}) %all-to-all-start.1) | async-done | bytes 1114144 | tf_op jit(solution)/shard_map/all_to_all | solution.py:509
  75.2 1.6 %shard_map.41 = f32[2048,128]{1,0:T(8,128)S(1)} custom-call(s32[256]{0:T(256)S(1)} %fusion.2.starts, f32[2176,128]{1,0:T(8,128)S(1)} %bitcast.29), custom_call_target="tpu_custom_call" | custom-call | tf_op jit(solution)/shard_map/pallas_call | solution.py:419
  76.9 18.8 %all_to_all.21 = f32[16,8,2,2,4,128]{5,4,3,2,1,0:T(4,128)S(1)} all-to-all(f32[16,8,2,2,4,128]{5,4,3,2,1,0:T(4,128)S(1)} %bitcast.31), channel_id=1, replica_groups=mesh['img'=16,'slab'=16] {'img'}, dimensions={0} | all-to-all | bytes 2097152 | tf_op jit(solution)/shard_map/all_to_all | solution.py:517
  95.6 1.2 %copy.12 = f32[8,2,16,2,4,128]{5,4,3,2,1,0:T(4,128)} copy(f32[8,2,16,2,4,128]{5,4,3,1,0,2:T(4,128)S(1)} %bitcast.32) | data formatting | bytes 2097152 | tf_op jit(solution)/shard_map/transpose | solution.py:518
  (11 shorter events, 0.1 us)
Async XLA Ops:
  0.0 5.8 %copy-start.5 = (f32[8,2,32,4,128]{4,3,2,1,0:T(4,128)S(1)}, f32[8,2,32,4,128]{4,3,2,1,0:T(4,128)}, u32[]{:S(2)}) copy-start(f32[8,2,32,4,128]{4,3,2,1,0:T(4,128)} %param.3) | copy-start | bytes 3145732
  1.2 6.2 %collective-permute-start = (f32[2,4,4,8,128]{4,3,2,1,0:T(8,128)S(1)}, f32[2,4,4,8,128]{4,3,2,1,0:T(8,128)S(1)}, u32[]{:S(2)}, u32[]{:S(2)}) collective-permute-start(f32[2,4,4,8,128]{4,3,2,1,0:T(8,128)S(1)} %get-tuple-element.24), channel_id=1, source_target_pairs={{0,1},{1,0},{2,3},{3,2},{4,5},{5,4},{6,7},{7,6},{8,9},{9,8},{10,11... | collective-permute-start | bytes 393224 | tf_op jit(solution)/shard_map/ppermute | solution.py:447
  5.1 2.4 %collective-permute-start.1 = (f32[2,4,4,8,128]{4,3,2,1,0:T(8,128)S(1)}, f32[2,4,4,8,128]{4,3,2,1,0:T(8,128)S(1)}, u32[]{:S(2)}, u32[]{:S(2)}) collective-permute-start(f32[2,4,4,8,128]{4,3,2,1,0:T(8,128)S(1)} %get-tuple-element.23), channel_id=1, source_target_pairs={{1,2},{2,1},{3,4},{4,3},{5,6},{6,5},{7,8},{8,7},{9,10},{10,9},{11,... | collective-permute-start | bytes 393224 | tf_op jit(solution)/shard_map/ppermute | solution.py:448
  7.4 10.3 %copy-start.1 = (f32[2,4,4,8,128]{4,3,2,1,0:T(8,128)}, f32[2,4,4,8,128]{4,3,2,1,0:T(8,128)S(1)}, u32[]{:S(2)}) copy-start(f32[2,4,4,8,128]{4,3,2,1,0:T(8,128)S(1)} %collective-permute-done.side_a) | copy-start | bytes 393220
  7.4 10.3 %copy-start.2 = (f32[2,4,4,8,128]{4,3,2,1,0:T(8,128)}, f32[2,4,4,8,128]{4,3,2,1,0:T(8,128)S(1)}, u32[]{:S(2)}) copy-start(f32[2,4,4,8,128]{4,3,2,1,0:T(8,128)S(1)} %collective-permute-done.1.side_b) | copy-start | bytes 393220
  7.6 9.4 %collective-permute-start.2 = (f32[288,128]{1,0:T(8,128)S(1)}, f32[288,128]{1,0:T(8,128)S(1)}, u32[]{:S(2)}, u32[]{:S(2)}) collective-permute-start(f32[288,128]{1,0:T(8,128)S(1)} %bitcast.34), channel_id=1, source_target_pairs={{0,16},{16,0},{32,48},{48,32},{64,80},{80,64},{96,112},{112,96},{1... | collective-permute-start | bytes 442376 | tf_op jit(solution)/shard_map/ppermute | solution.py:465
  11.3 6.5 %collective-permute-start.3 = (f32[288,128]{1,0:T(8,128)S(1)}, f32[288,128]{1,0:T(8,128)S(1)}, u32[]{:S(2)}, u32[]{:S(2)}) collective-permute-start(f32[288,128]{1,0:T(8,128)S(1)} %bitcast.33), channel_id=1, source_target_pairs={{16,32},{32,16},{48,64},{64,48},{80,96},{96,80},{112,128},{128,112... | collective-permute-start | bytes 442376 | tf_op jit(solution)/shard_map/ppermute | solution.py:466
  17.0 2.9 %copy-start = (f32[4,2,32,4,8,128]{5,4,3,2,1,0:T(8,128)}, f32[4,2,32,4,8,128]{5,4,3,2,1,0:T(8,128)S(1)}, u32[]{:S(2)}) copy-start(f32[4,2,32,4,8,128]{5,4,3,2,1,0:T(8,128)S(1)} %shard_map.37.fields.given) | copy-start | bytes 12582916
  17.0 2.9 %copy-start.3 = (f32[288,128]{1,0:T(8,128)}, f32[288,128]{1,0:T(8,128)S(1)}, u32[]{:S(2)}) copy-start(f32[288,128]{1,0:T(8,128)S(1)} %collective-permute-done.2.image_a) | copy-start | bytes 442372
  17.7 2.2 %copy-start.4 = (f32[288,128]{1,0:T(8,128)}, f32[288,128]{1,0:T(8,128)S(1)}, u32[]{:S(2)}) copy-start(f32[288,128]{1,0:T(8,128)S(1)} %collective-permute-done.3.image_b) | copy-start | bytes 442372
  19.9 23.1 %all-to-all-start = ((f32[16,1,128]{2,1,0:T(1,128)}), f32[16,1,128]{2,1,0:T(1,128)S(1)}, u32[]{:S(2)}, u32[]{:S(2)}) async-start(f32[16,1,128]{2,1,0:T(1,128)} %bitcast.14), calls=%async_computation | async-start | bytes 16384 | tf_op jit(solution)/shard_map/all_to_all | solution.py:484
  43.0 0.6 copy-start.6
  52.7 5.9 %copy-start.7 = (s32[128,2]{0,1:T(2,128)S(1)}, s32[128,2]{0,1:T(2,128)}, u32[]{:S(2)}) copy-start(s32[128,2]{0,1:T(2,128)} %param.4) | copy-start | bytes 3076
  52.7 22.5 %all-to-all-start.1 = ((f32[16,136,128]{2,1,0:T(8,128)}), f32[16,136,128]{2,1,0:T(8,128)S(1)}, u32[]{:S(2)}, u32[]{:S(2)}) async-start(f32[16,136,128]{2,1,0:T(8,128)} %shard_map.40), calls=%async_computation.1 | async-start | bytes 2228224 | tf_op jit(solution)/shard_map/all_to_all | solution.py:509

commit v4 on v3

--- a/solution.py
+++ b/solution.py
@@ -165,8 +165,14 @@
 
 
 def layer_of(depth, body, side):
+    low_open, high_open = ends_open()
+
     def phi(z):
-        return load(side.at[0], z + 4) if z < 0 else load(side.at[1], z - depth) if z >= depth else load(body, z)
+        if z < 0:
+            return each(lambda v: jnp.where(low_open > 0.0, v, 0.0), load(side.at[0], z + 4))
+        if z >= depth:
+            return each(lambda v: jnp.where(high_open > 0.0, v, 0.0), load(side.at[1], z - depth))
+        return load(body, z)
 
     return phi
 
@@ -250,7 +256,8 @@
 
 
 def update_kernel(depth, images, given, diff_given, both_given, rim_mu_given, rim_half_given, rim_own_given, *refs):
-    sums, level, out, m_ref, bar, inner, fields, diff, both, rim_mu, rim_half, rim_own, sems = refs
+    sums_given, level, out, m_ref, bar, inner, fields, diff, both, rim_mu, rim_half, rim_own, sums, sems = refs
+    sums_here = fetch([(sums_given, sums)], sems.at[5])
     cut = depth // 4
     parts = [(2, cut), (cut, depth - 2)]
     rim_here = fetch(
@@ -287,6 +294,7 @@
     slot, drift_slot = rim_layers(depth)
     sub = lax.broadcasted_iota(jnp.int32, (8, 128), 0)
     lane = lax.broadcasted_iota(jnp.int32, (8, 128), 1)
+    sums_here()
     added = jnp.sum(sums[...], axis=0, keepdims=True)
     drift_sq = jnp.sum(jnp.where(lane == sub, added, 0.0), axis=1, keepdims=True)
     tangent_sq = jnp.sum(jnp.where(lane == sub + 8, added, 0.0), axis=1, keepdims=True)
@@ -429,7 +437,7 @@
 
 def swaps(count):
     near = [(i, i ^ 1) for i in range(count)]
-    far = [pair for i in range(1, count - 1, 2) for pair in ((i, i + 1), (i + 1, i))]
+    far = [pair for i in range(1, count, 2) for pair in ((i, (i + 1) % count), ((i + 1) % count, i))]
     return near, far
 
 
@@ -447,6 +455,7 @@
     side_a = lax.ppermute(jnp.where(even_slab, top, bottom), "slab", near)
     side_b = lax.ppermute(jnp.where(even_slab, bottom, top), "slab", far)
     body = lax.optimization_barrier(state).transpose(1, 2, 3, 0, 4)
+    side_a, side_b, body = lax.optimization_barrier((side_a, side_b, body))
     fields = call(
         functools.partial(drift_kernel, depth),
         (body,),
@@ -498,12 +507,12 @@
     updated = call(
         functools.partial(update_kernel, depth, images),
         (fields, *prepared, sums, weight_index),
-        [ANY] * 6 + [VMEM, SMEM],
+        [ANY] * 7 + [SMEM],
         jax.ShapeDtypeStruct((depth // 2, (rows + 1) * 8, 128), F32),
         [pltpu.VMEM(wide, F32)]
         + [pltpu.VMEM(layers(depth + 2), F32)] * 2
-        + [pltpu.VMEM(array.shape, F32) for array in (fields, *prepared)]
-        + [pltpu.SemaphoreType.DMA((5, 4))],
+        + [pltpu.VMEM(array.shape, F32) for array in (fields, *prepared, sums)]
+        + [pltpu.SemaphoreType.DMA((6, 4))],
         limit=MOST,
     )
     got = lax.all_to_all(updated, "img", 0, 0, tiled=True)

time: 97.3 us -> 94.6 us (0.972)
  starting transfers between devices: 30.2 us -> 27.3 us
    all_to_all x1, starting transfers between devices: 14.2 us -> 8.41 us  [local(): sums = lax.all_to_all(sums, 'slab', 0, 0, tiled=True)]
    ppermute x1, starting transfers between devices: 0.66 us -> 5.39 us  [local(): side_b = lax.ppermute(jnp.where(even_slab, bottom, top), 'slab', far)]
    ppermute x1, waiting for transfers between devices: 0.01 us -> 2.27 us  [local(): side_b = lax.ppermute(jnp.where(even_slab, bottom, top), 'slab', far)]
    ppermute x1, starting transfers between devices: 3.7 us -> 1.6 us  [local(): image_a = lax.ppermute(jnp.where(even_img, ends[1], ends[0]), 'img', near)]
    ppermute x1, waiting for transfers between devices: 1.64 us -> 0.01 us  [local(): side_a = lax.ppermute(jnp.where(even_slab, top, bottom), 'slab', near)]
where the time goes in v4:
time: 94.6 us; the launch traced here: 94.3 us
  starting transfers between devices  27.3 us (29%)
  waiting for transfers between devices  23.7 us (25%)
  Pallas kernels  20.5 us (22%)
  blocking collectives  18.7 us (20%)
  local copies, waits for them, and re-layouts  3.6 us (4%)
    pallas_call x5, Pallas kernels, call(): pl.pallas_call(kernel, in_specs=in_specs, out_specs=jax.tree.map(lambda _...  20.5 us
    all_to_all x1, blocking collectives, local(): lax.all_to_all(new.reshape(img_count, per_dev, 2, 2, GX, 128), 'img', 0,...  18.7 us
    all_to_all x1, waiting for transfers between devices, local(): got = lax.all_to_all(updated, 'img', 0, 0, tiled=True)  16.6 us
    all_to_all x1, starting transfers between devices, local(): sums = lax.all_to_all(sums, 'slab', 0, 0, tiled=True)  8.41 us
    all_to_all x1, starting transfers between devices, local(): got = lax.all_to_all(updated, 'img', 0, 0, tiled=True)  6.89 us
    ppermute x1, starting transfers between devices, local(): side_b = lax.ppermute(jnp.where(even_slab, bottom, top), 'slab', far)  5.39 us
    all_to_all x1, waiting for transfers between devices, local(): sums = lax.all_to_all(sums, 'slab', 0, 0, tiled=True)  4.36 us
    ppermute x1, starting transfers between devices, local(): side_a = lax.ppermute(jnp.where(even_slab, top, bottom), 'slab', near)  3.83 us
  transfers between devices with their start and end apart: 6, of which 4 were waited for; matrix products, arithmetic and copies ran while one was open for 1% of the time, Pallas kernels for 8%

profile of v4, /device:TPU:1, one launch (start us, length us, event | category | flops | bytes accessed | tf_op | source)
XLA Modules:
  0.0 94.3 jit_solution(9214139126222651407)
XLA Ops:
  0.0 1.1 %fusion.3 = (f32[8,2,4,4,128]{4,3,2,1,0:T(4,128)S(1)}, f32[8,2,4,4,128]{4,3,2,1,0:T(4,128)S(1)}) fusion(f32[8,2,32,4,128]{4,3,2,1,0:T(4,128)} %param.3), kind=kLoop, calls=%fused_computation.19 | loop fusion | bytes 524288 | tf_op jit(solution)/shard_map/slice | solution.py:453
  1.1 0.2 select_bitcast_fusion
  1.2 3.8 %collective-permute-start = (f32[2,4,4,8,128]{4,3,2,1,0:T(8,128)S(1)}, f32[2,4,4,8,128]{4,3,2,1,0:T(8,128)S(1)}, u32[]{:S(2)}, u32[]{:S(2)}) collective-permute-start(f32[2,4,4,8,128]{4,3,2,1,0:T(8,128)S(1)} %get-tuple-element.30), channel_id=1, source_target_pairs={{0,1},{1,0},{2,3},{3,2},{4,5},{5,4},{6,7},{7,6},{8,9},{9,8},{10,11... | collective-permute-start | bytes 393224 | tf_op jit(solution)/shard_map/ppermute | solution.py:455
  5.1 5.4 %collective-permute-start.1 = (f32[2,4,4,8,128]{4,3,2,1,0:T(8,128)S(1)}, f32[2,4,4,8,128]{4,3,2,1,0:T(8,128)S(1)}, u32[]{:S(2)}, u32[]{:S(2)}) collective-permute-start(f32[2,4,4,8,128]{4,3,2,1,0:T(8,128)S(1)} %get-tuple-element.29), channel_id=1, source_target_pairs={{1,2},{2,1},{3,4},{4,3},{5,6},{6,5},{7,8},{8,7},{9,10},{10,9},{11,... | collective-permute-start | bytes 393224 | tf_op jit(solution)/shard_map/ppermute | solution.py:456
  10.5 0.0 copy-done.5
  10.5 0.6 copy.20
  11.1 0.0 collective-permute-done.side_a
  11.1 0.0 copy-start.1
  11.1 2.3 %collective-permute-done.1.side_b = f32[2,4,4,8,128]{4,3,2,1,0:T(8,128)S(1)} collective-permute-done((f32[2,4,4,8,128]{4,3,2,1,0:T(8,128)S(1)}, f32[2,4,4,8,128]{4,3,2,1,0:T(8,128)S(1)}, u32[]{:S(2)}, u32[]{:S(2)}) %collective-permute-start.1) | collective-permute-done | bytes 131104 | tf_op jit(solution)/shard_map/ppermute | solution.py:456
  13.5 0.1 broadcast_select_fusion
  13.5 1.6 %collective-permute-start.2 = (f32[288,128]{1,0:T(8,128)S(1)}, f32[288,128]{1,0:T(8,128)S(1)}, u32[]{:S(2)}, u32[]{:S(2)}) collective-permute-start(f32[288,128]{1,0:T(8,128)S(1)} %bitcast.34), channel_id=1, source_target_pairs={{0,16},{16,0},{32,48},{48,32},{64,80},{80,64},{96,112},{112,96},{1... | collective-permute-start | bytes 442376 | tf_op jit(solution)/shard_map/ppermute | solution.py:474
  15.1 1.2 %collective-permute-start.3 = (f32[288,128]{1,0:T(8,128)S(1)}, f32[288,128]{1,0:T(8,128)S(1)}, u32[]{:S(2)}, u32[]{:S(2)}) collective-permute-start(f32[288,128]{1,0:T(8,128)S(1)} %bitcast.33), channel_id=1, source_target_pairs={{16,32},{32,16},{48,64},{64,48},{80,96},{96,80},{112,128},{128,112... | collective-permute-start | bytes 442376 | tf_op jit(solution)/shard_map/ppermute | solution.py:475
  16.3 3.2 %shard_map.37.fields.given = f32[4,2,32,4,8,128]{5,4,3,2,1,0:T(8,128)S(1)} custom-call(f32[2,32,4,8,128]{4,3,2,1,0:T(8,128)S(1)} %bitcast.30), custom_call_target="tpu_custom_call" | custom-call | flops 16000000 | bytes 4000000 | tf_op jit(solution)/shard_map/pallas_call | solution.py:427
  19.5 0.0 collective-permute-done.2.image_a
  19.5 0.0 copy-start.3
  19.5 0.5 collective-permute-done.3.image_b
  20.0 2.2 %shard_map.39 = f32[16,128]{1,0:T(8,128)} custom-call(f32[2,4,4,8,128]{4,3,2,1,0:T(8,128)S(1)} %collective-permute-done.side_a, f32[2,4,4,8,128]{4,3,2,1,0:T(8,128)S(1)} %collective-permute-done.1.side_b, f32[288,128]{1,0:T(8,128)S(1)} %collective-permute-done.2.image_a, f32[288,128]{1,0:T(8,128)S(1)} %collective-permute-done.3.image_b, ...), custom_call_target="tpu_custom_call" | custom-call | tf_op jit(solution)/shard_map/pallas_call | solution.py:427
  22.2 0.0 copy-done
  22.2 0.0 copy-done.3
  22.2 0.0 copy-done.4
  22.2 8.4 %all-to-all-start = ((f32[16,1,128]{2,1,0:T(1,128)}), f32[16,1,128]{2,1,0:T(1,128)S(1)}, u32[]{:S(2)}, u32[]{:S(2)}) async-start(f32[16,1,128]{2,1,0:T(1,128)} %bitcast.14), calls=%async_computation | async-start | bytes 16384 | tf_op jit(solution)/shard_map/all_to_all | solution.py:493
  30.6 4.5 %shard_map.38 = (f32[2,36,4,8,128]{4,3,2,1,0:T(8,128)}, f32[2,36,4,8,128]{4,3,2,1,0:T(8,128)}, f32[2,6,4,8,128]{4,3,2,1,0:T(8,128)}, f32[2,6,4,8,128]{4,3,2,1,0:T(8,128)}, f32[2,8,4,8,128]{4,3,2,1,0:T(8,128)}) custom-call(f32[2,4,4,8,128]{4,3,2,1,0:T(8,128)} %copy-done.1, f32[2,4,4,8,128]{4,3,2,1,0:T(8,128)} %copy-done.2, f32[288,128]{1,0:T(8,128)} %copy-done.3, ...), custom_call_target="tpu_custom_call" | custom-call | flops 8000000 | bytes 4000000 | tf_op jit(solution)/shard_map/pallas_call | solution.py:427
  35.2 4.4 %all-to-all-done = f32[16,1,128]{2,1,0:T(1,128)S(1)} async-done(((f32[16,1,128]{2,1,0:T(1,128)}), f32[16,1,128]{2,1,0:T(1,128)S(1)}, u32[]{:S(2)}, u32[]{:S(2)}) %all-to-all-start) | async-done | bytes 8224 | tf_op jit(solution)/shard_map/all_to_all | solution.py:493
  39.5 0.6 copy-done.6
  40.1 9.0 %shard_map.40 = f32[16,136,128]{2,1,0:T(8,128)} custom-call(f32[4,2,32,4,8,128]{5,4,3,2,1,0:T(8,128)} %copy-done, f32[2,36,4,8,128]{4,3,2,1,0:T(8,128)} %get-tuple-element.16.diff_given, f32[2,36,4,8,128]{4,3,2,1,0:T(8,128)} %get-tuple-element.17.both_given, f32[2,6,4,8,128]{4,3,2,1,0:T(8,128)} %get-tuple-element.18.rim_mu_given, ...), custom_call_target="tpu_custom_call" | custom-call | tf_op jit(solution)/shard_map/pallas_call | solution.py:427
  49.1 0.0 copy-start.7
  49.2 6.9 %all-to-all-start.1 = ((f32[16,136,128]{2,1,0:T(8,128)}), f32[16,136,128]{2,1,0:T(8,128)S(1)}, u32[]{:S(2)}, u32[]{:S(2)}) async-start(f32[16,136,128]{2,1,0:T(8,128)} %shard_map.40), calls=%async_computation.1 | async-start | bytes 2228224 | tf_op jit(solution)/shard_map/all_to_all | solution.py:518
  56.0 0.0 copy-done.7
  56.1 16.6 %all-to-all-done.1 = f32[16,136,128]{2,1,0:T(8,128)S(1)} async-done(((f32[16,136,128]{2,1,0:T(8,128)}), f32[16,136,128]{2,1,0:T(8,128)S(1)}, u32[]{:S(2)}, u32[]{:S(2)}) %all-to-all-start.1) | async-done | bytes 1114144 | tf_op jit(solution)/shard_map/all_to_all | solution.py:518
  72.7 1.6 %shard_map.41 = f32[2048,128]{1,0:T(8,128)S(1)} custom-call(s32[256]{0:T(256)S(1)} %fusion.2.starts, f32[2176,128]{1,0:T(8,128)S(1)} %bitcast.29), custom_call_target="tpu_custom_call" | custom-call | tf_op jit(solution)/shard_map/pallas_call | solution.py:427
  74.3 18.7 %all_to_all.21 = f32[16,8,2,2,4,128]{5,4,3,2,1,0:T(4,128)S(1)} all-to-all(f32[16,8,2,2,4,128]{5,4,3,2,1,0:T(4,128)S(1)} %bitcast.31), channel_id=1, replica_groups=mesh['img'=16,'slab'=16] {'img'}, dimensions={0} | all-to-all | bytes 2097152 | tf_op jit(solution)/shard_map/all_to_all | solution.py:526
  93.1 1.2 %copy.12 = f32[8,2,16,2,4,128]{5,4,3,2,1,0:T(4,128)} copy(f32[8,2,16,2,4,128]{5,4,3,1,0,2:T(4,128)S(1)} %bitcast.32) | data formatting | bytes 2097152 | tf_op jit(solution)/shard_map/transpose | solution.py:527
  (11 shorter events, 0.1 us)
Async XLA Ops:
  0.0 10.5 %copy-start.5 = (f32[8,2,32,4,128]{4,3,2,1,0:T(4,128)S(1)}, f32[8,2,32,4,128]{4,3,2,1,0:T(4,128)}, u32[]{:S(2)}) copy-start(f32[8,2,32,4,128]{4,3,2,1,0:T(4,128)} %param.3) | copy-start | bytes 3145732
  1.2 9.9 %collective-permute-start = (f32[2,4,4,8,128]{4,3,2,1,0:T(8,128)S(1)}, f32[2,4,4,8,128]{4,3,2,1,0:T(8,128)S(1)}, u32[]{:S(2)}, u32[]{:S(2)}) collective-permute-start(f32[2,4,4,8,128]{4,3,2,1,0:T(8,128)S(1)} %get-tuple-element.30), channel_id=1, source_target_pairs={{0,1},{1,0},{2,3},{3,2},{4,5},{5,4},{6,7},{7,6},{8,9},{9,8},{10,11... | collective-permute-start | bytes 393224 | tf_op jit(solution)/shard_map/ppermute | solution.py:455
  5.1 8.3 %collective-permute-start.1 = (f32[2,4,4,8,128]{4,3,2,1,0:T(8,128)S(1)}, f32[2,4,4,8,128]{4,3,2,1,0:T(8,128)S(1)}, u32[]{:S(2)}, u32[]{:S(2)}) collective-permute-start(f32[2,4,4,8,128]{4,3,2,1,0:T(8,128)S(1)} %get-tuple-element.29), channel_id=1, source_target_pairs={{1,2},{2,1},{3,4},{4,3},{5,6},{6,5},{7,8},{8,7},{9,10},{10,9},{11,... | collective-permute-start | bytes 393224 | tf_op jit(solution)/shard_map/ppermute | solution.py:456
  11.1 8.9 %copy-start.1 = (f32[2,4,4,8,128]{4,3,2,1,0:T(8,128)}, f32[2,4,4,8,128]{4,3,2,1,0:T(8,128)S(1)}, u32[]{:S(2)}) copy-start(f32[2,4,4,8,128]{4,3,2,1,0:T(8,128)S(1)} %collective-permute-done.side_a) | copy-start | bytes 393220
  13.4 6.6 %copy-start.2 = (f32[2,4,4,8,128]{4,3,2,1,0:T(8,128)}, f32[2,4,4,8,128]{4,3,2,1,0:T(8,128)S(1)}, u32[]{:S(2)}) copy-start(f32[2,4,4,8,128]{4,3,2,1,0:T(8,128)S(1)} %collective-permute-done.1.side_b) | copy-start | bytes 393220
  13.5 6.0 %collective-permute-start.2 = (f32[288,128]{1,0:T(8,128)S(1)}, f32[288,128]{1,0:T(8,128)S(1)}, u32[]{:S(2)}, u32[]{:S(2)}) collective-permute-start(f32[288,128]{1,0:T(8,128)S(1)} %bitcast.34), channel_id=1, source_target_pairs={{0,16},{16,0},{32,48},{48,32},{64,80},{80,64},{96,112},{112,96},{1... | collective-permute-start | bytes 442376 | tf_op jit(solution)/shard_map/ppermute | solution.py:474
  15.1 4.9 %collective-permute-start.3 = (f32[288,128]{1,0:T(8,128)S(1)}, f32[288,128]{1,0:T(8,128)S(1)}, u32[]{:S(2)}, u32[]{:S(2)}) collective-permute-start(f32[288,128]{1,0:T(8,128)S(1)} %bitcast.33), channel_id=1, source_target_pairs={{16,32},{32,16},{48,64},{64,48},{80,96},{96,80},{112,128},{128,112... | collective-permute-start | bytes 442376 | tf_op jit(solution)/shard_map/ppermute | solution.py:475
  19.5 2.7 %copy-start = (f32[4,2,32,4,8,128]{5,4,3,2,1,0:T(8,128)}, f32[4,2,32,4,8,128]{5,4,3,2,1,0:T(8,128)S(1)}, u32[]{:S(2)}) copy-start(f32[4,2,32,4,8,128]{5,4,3,2,1,0:T(8,128)S(1)} %shard_map.37.fields.given) | copy-start | bytes 12582916
  19.5 2.7 %copy-start.3 = (f32[288,128]{1,0:T(8,128)}, f32[288,128]{1,0:T(8,128)S(1)}, u32[]{:S(2)}) copy-start(f32[288,128]{1,0:T(8,128)S(1)} %collective-permute-done.2.image_a) | copy-start | bytes 442372
  20.0 2.2 %copy-start.4 = (f32[288,128]{1,0:T(8,128)}, f32[288,128]{1,0:T(8,128)S(1)}, u32[]{:S(2)}) copy-start(f32[288,128]{1,0:T(8,128)S(1)} %collective-permute-done.3.image_b) | copy-start | bytes 442372
  22.2 17.3 %all-to-all-start = ((f32[16,1,128]{2,1,0:T(1,128)}), f32[16,1,128]{2,1,0:T(1,128)S(1)}, u32[]{:S(2)}, u32[]{:S(2)}) async-start(f32[16,1,128]{2,1,0:T(1,128)} %bitcast.14), calls=%async_computation | async-start | bytes 16384 | tf_op jit(solution)/shard_map/all_to_all | solution.py:493
  39.5 0.6 copy-start.6
  49.1 6.9 %copy-start.7 = (s32[128,2]{0,1:T(2,128)S(1)}, s32[128,2]{0,1:T(2,128)}, u32[]{:S(2)}) copy-start(s32[128,2]{0,1:T(2,128)} %param.4) | copy-start | bytes 3076
  49.2 23.5 %all-to-all-start.1 = ((f32[16,136,128]{2,1,0:T(8,128)}), f32[16,136,128]{2,1,0:T(8,128)S(1)}, u32[]{:S(2)}, u32[]{:S(2)}) async-start(f32[16,136,128]{2,1,0:T(8,128)} %shard_map.40), calls=%async_computation.1 | async-start | bytes 2228224 | tf_op jit(solution)/shard_map/all_to_all | solution.py:518

commit v5 on v4

--- a/solution.py
+++ b/solution.py
@@ -92,7 +92,7 @@
         store(half, z, h)
         return carry
 
-    lax.fori_loop(1, depth - 1, first_fields, 0, unroll=2)
+    lax.fori_loop(1, depth - 1, first_fields, 0, unroll=3)
 
     def flux(z, lower):
         p, h = load(mu, z), load(half, z)

time: 94.6 us -> 94.6 us (level)
  no operation moved by 1% of the time
where the time goes in v5:
time: 94.6 us; the launch traced here: 94.3 us
  starting transfers between devices  27.3 us (29%)
  waiting for transfers between devices  24.1 us (25%)
  Pallas kernels  20.2 us (21%)
  blocking collectives  18.7 us (20%)
  local copies, waits for them, and re-layouts  3.6 us (4%)
    pallas_call x5, Pallas kernels, call(): pl.pallas_call(kernel, in_specs=in_specs, out_specs=jax.tree.map(lambda _...  20.2 us
    all_to_all x1, blocking collectives, local(): lax.all_to_all(new.reshape(img_count, per_dev, 2, 2, GX, 128), 'img', 0,...  18.7 us
    all_to_all x1, waiting for transfers between devices, local(): got = lax.all_to_all(updated, 'img', 0, 0, tiled=True)  16.6 us
    all_to_all x1, starting transfers between devices, local(): sums = lax.all_to_all(sums, 'slab', 0, 0, tiled=True)  8.41 us
    all_to_all x1, starting transfers between devices, local(): got = lax.all_to_all(updated, 'img', 0, 0, tiled=True)  6.83 us
    ppermute x1, starting transfers between devices, local(): side_b = lax.ppermute(jnp.where(even_slab, bottom, top), 'slab', far)  5.39 us
    all_to_all x1, waiting for transfers between devices, local(): sums = lax.all_to_all(sums, 'slab', 0, 0, tiled=True)  4.36 us
    ppermute x1, starting transfers between devices, local(): side_a = lax.ppermute(jnp.where(even_slab, top, bottom), 'slab', near)  3.83 us
  transfers between devices with their start and end apart: 6, of which 4 were waited for; matrix products, arithmetic and copies ran while one was open for 1% of the time, Pallas kernels for 8%

profile of v5, /device:TPU:1, one launch (start us, length us, event | category | flops | bytes accessed | tf_op | source)
XLA Modules:
  0.0 94.3 jit_solution(6748250370300323306)
XLA Ops:
  0.0 1.1 %fusion.3 = (f32[8,2,4,4,128]{4,3,2,1,0:T(4,128)S(1)}, f32[8,2,4,4,128]{4,3,2,1,0:T(4,128)S(1)}) fusion(f32[8,2,32,4,128]{4,3,2,1,0:T(4,128)} %param.3), kind=kLoop, calls=%fused_computation.19 | loop fusion | bytes 524288 | tf_op jit(solution)/shard_map/slice | solution.py:453
  1.1 0.2 select_bitcast_fusion
  1.2 3.8 %collective-permute-start = (f32[2,4,4,8,128]{4,3,2,1,0:T(8,128)S(1)}, f32[2,4,4,8,128]{4,3,2,1,0:T(8,128)S(1)}, u32[]{:S(2)}, u32[]{:S(2)}) collective-permute-start(f32[2,4,4,8,128]{4,3,2,1,0:T(8,128)S(1)} %get-tuple-element.30), channel_id=1, source_target_pairs={{0,1},{1,0},{2,3},{3,2},{4,5},{5,4},{6,7},{7,6},{8,9},{9,8},{10,11... | collective-permute-start | bytes 393224 | tf_op jit(solution)/shard_map/ppermute | solution.py:455
  5.1 5.4 %collective-permute-start.1 = (f32[2,4,4,8,128]{4,3,2,1,0:T(8,128)S(1)}, f32[2,4,4,8,128]{4,3,2,1,0:T(8,128)S(1)}, u32[]{:S(2)}, u32[]{:S(2)}) collective-permute-start(f32[2,4,4,8,128]{4,3,2,1,0:T(8,128)S(1)} %get-tuple-element.29), channel_id=1, source_target_pairs={{1,2},{2,1},{3,4},{4,3},{5,6},{6,5},{7,8},{8,7},{9,10},{10,9},{11,... | collective-permute-start | bytes 393224 | tf_op jit(solution)/shard_map/ppermute | solution.py:456
  10.5 0.0 copy-done.5
  10.5 0.6 copy.20
  11.1 0.0 collective-permute-done.side_a
  11.1 0.0 copy-start.1
  11.1 2.3 %collective-permute-done.1.side_b = f32[2,4,4,8,128]{4,3,2,1,0:T(8,128)S(1)} collective-permute-done((f32[2,4,4,8,128]{4,3,2,1,0:T(8,128)S(1)}, f32[2,4,4,8,128]{4,3,2,1,0:T(8,128)S(1)}, u32[]{:S(2)}, u32[]{:S(2)}) %collective-permute-start.1) | collective-permute-done | bytes 131104 | tf_op jit(solution)/shard_map/ppermute | solution.py:456
  13.5 0.1 broadcast_select_fusion
  13.5 1.6 %collective-permute-start.2 = (f32[288,128]{1,0:T(8,128)S(1)}, f32[288,128]{1,0:T(8,128)S(1)}, u32[]{:S(2)}, u32[]{:S(2)}) collective-permute-start(f32[288,128]{1,0:T(8,128)S(1)} %bitcast.34), channel_id=1, source_target_pairs={{0,16},{16,0},{32,48},{48,32},{64,80},{80,64},{96,112},{112,96},{1... | collective-permute-start | bytes 442376 | tf_op jit(solution)/shard_map/ppermute | solution.py:474
  15.1 1.2 %collective-permute-start.3 = (f32[288,128]{1,0:T(8,128)S(1)}, f32[288,128]{1,0:T(8,128)S(1)}, u32[]{:S(2)}, u32[]{:S(2)}) collective-permute-start(f32[288,128]{1,0:T(8,128)S(1)} %bitcast.33), channel_id=1, source_target_pairs={{16,32},{32,16},{48,64},{64,48},{80,96},{96,80},{112,128},{128,112... | collective-permute-start | bytes 442376 | tf_op jit(solution)/shard_map/ppermute | solution.py:475
  16.3 2.8 %shard_map.37.fields.given = f32[4,2,32,4,8,128]{5,4,3,2,1,0:T(8,128)S(1)} custom-call(f32[2,32,4,8,128]{4,3,2,1,0:T(8,128)S(1)} %bitcast.30), custom_call_target="tpu_custom_call" | custom-call | flops 16000000 | bytes 4000000 | tf_op jit(solution)/shard_map/pallas_call | solution.py:427
  19.2 0.0 collective-permute-done.2.image_a
  19.2 0.0 copy-start.3
  19.2 0.8 collective-permute-done.3.image_b
  20.0 2.2 %shard_map.39 = f32[16,128]{1,0:T(8,128)} custom-call(f32[2,4,4,8,128]{4,3,2,1,0:T(8,128)S(1)} %collective-permute-done.side_a, f32[2,4,4,8,128]{4,3,2,1,0:T(8,128)S(1)} %collective-permute-done.1.side_b, f32[288,128]{1,0:T(8,128)S(1)} %collective-permute-done.2.image_a, f32[288,128]{1,0:T(8,128)S(1)} %collective-permute-done.3.image_b, ...), custom_call_target="tpu_custom_call" | custom-call | tf_op jit(solution)/shard_map/pallas_call | solution.py:427
  22.2 0.0 copy-done
  22.2 0.0 copy-done.3
  22.2 0.0 copy-done.4
  22.2 8.4 %all-to-all-start = ((f32[16,1,128]{2,1,0:T(1,128)}), f32[16,1,128]{2,1,0:T(1,128)S(1)}, u32[]{:S(2)}, u32[]{:S(2)}) async-start(f32[16,1,128]{2,1,0:T(1,128)} %bitcast.14), calls=%async_computation | async-start | bytes 16384 | tf_op jit(solution)/shard_map/all_to_all | solution.py:493
  30.6 4.5 %shard_map.38 = (f32[2,36,4,8,128]{4,3,2,1,0:T(8,128)}, f32[2,36,4,8,128]{4,3,2,1,0:T(8,128)}, f32[2,6,4,8,128]{4,3,2,1,0:T(8,128)}, f32[2,6,4,8,128]{4,3,2,1,0:T(8,128)}, f32[2,8,4,8,128]{4,3,2,1,0:T(8,128)}) custom-call(f32[2,4,4,8,128]{4,3,2,1,0:T(8,128)} %copy-done.1, f32[2,4,4,8,128]{4,3,2,1,0:T(8,128)} %copy-done.2, f32[288,128]{1,0:T(8,128)} %copy-done.3, ...), custom_call_target="tpu_custom_call" | custom-call | flops 8000000 | bytes 4000000 | tf_op jit(solution)/shard_map/pallas_call | solution.py:427
  35.2 4.4 %all-to-all-done = f32[16,1,128]{2,1,0:T(1,128)S(1)} async-done(((f32[16,1,128]{2,1,0:T(1,128)}), f32[16,1,128]{2,1,0:T(1,128)S(1)}, u32[]{:S(2)}, u32[]{:S(2)}) %all-to-all-start) | async-done | bytes 8224 | tf_op jit(solution)/shard_map/all_to_all | solution.py:493
  39.5 0.6 copy-done.6
  40.1 9.0 %shard_map.40 = f32[16,136,128]{2,1,0:T(8,128)} custom-call(f32[4,2,32,4,8,128]{5,4,3,2,1,0:T(8,128)} %copy-done, f32[2,36,4,8,128]{4,3,2,1,0:T(8,128)} %get-tuple-element.16.diff_given, f32[2,36,4,8,128]{4,3,2,1,0:T(8,128)} %get-tuple-element.17.both_given, f32[2,6,4,8,128]{4,3,2,1,0:T(8,128)} %get-tuple-element.18.rim_mu_given, ...), custom_call_target="tpu_custom_call" | custom-call | tf_op jit(solution)/shard_map/pallas_call | solution.py:427
  49.1 0.0 copy-start.7
  49.2 6.8 %all-to-all-start.1 = ((f32[16,136,128]{2,1,0:T(8,128)}), f32[16,136,128]{2,1,0:T(8,128)S(1)}, u32[]{:S(2)}, u32[]{:S(2)}) async-start(f32[16,136,128]{2,1,0:T(8,128)} %shard_map.40), calls=%async_computation.1 | async-start | bytes 2228224 | tf_op jit(solution)/shard_map/all_to_all | solution.py:518
  56.0 0.0 copy-done.7
  56.0 16.6 %all-to-all-done.1 = f32[16,136,128]{2,1,0:T(8,128)S(1)} async-done(((f32[16,136,128]{2,1,0:T(8,128)}), f32[16,136,128]{2,1,0:T(8,128)S(1)}, u32[]{:S(2)}, u32[]{:S(2)}) %all-to-all-start.1) | async-done | bytes 1114144 | tf_op jit(solution)/shard_map/all_to_all | solution.py:518
  72.6 1.6 %shard_map.41 = f32[2048,128]{1,0:T(8,128)S(1)} custom-call(s32[256]{0:T(256)S(1)} %fusion.2.starts, f32[2176,128]{1,0:T(8,128)S(1)} %bitcast.29), custom_call_target="tpu_custom_call" | custom-call | tf_op jit(solution)/shard_map/pallas_call | solution.py:427
  74.3 18.7 %all_to_all.21 = f32[16,8,2,2,4,128]{5,4,3,2,1,0:T(4,128)S(1)} all-to-all(f32[16,8,2,2,4,128]{5,4,3,2,1,0:T(4,128)S(1)} %bitcast.31), channel_id=1, replica_groups=mesh['img'=16,'slab'=16] {'img'}, dimensions={0} | all-to-all | bytes 2097152 | tf_op jit(solution)/shard_map/all_to_all | solution.py:526
  93.0 1.2 %copy.12 = f32[8,2,16,2,4,128]{5,4,3,2,1,0:T(4,128)} copy(f32[8,2,16,2,4,128]{5,4,3,1,0,2:T(4,128)S(1)} %bitcast.32) | data formatting | bytes 2097152 | tf_op jit(solution)/shard_map/transpose | solution.py:527
  (11 shorter events, 0.1 us)
Async XLA Ops:
  0.0 10.5 %copy-start.5 = (f32[8,2,32,4,128]{4,3,2,1,0:T(4,128)S(1)}, f32[8,2,32,4,128]{4,3,2,1,0:T(4,128)}, u32[]{:S(2)}) copy-start(f32[8,2,32,4,128]{4,3,2,1,0:T(4,128)} %param.3) | copy-start | bytes 3145732
  1.2 9.9 %collective-permute-start = (f32[2,4,4,8,128]{4,3,2,1,0:T(8,128)S(1)}, f32[2,4,4,8,128]{4,3,2,1,0:T(8,128)S(1)}, u32[]{:S(2)}, u32[]{:S(2)}) collective-permute-start(f32[2,4,4,8,128]{4,3,2,1,0:T(8,128)S(1)} %get-tuple-element.30), channel_id=1, source_target_pairs={{0,1},{1,0},{2,3},{3,2},{4,5},{5,4},{6,7},{7,6},{8,9},{9,8},{10,11... | collective-permute-start | bytes 393224 | tf_op jit(solution)/shard_map/ppermute | solution.py:455
  5.1 8.3 %collective-permute-start.1 = (f32[2,4,4,8,128]{4,3,2,1,0:T(8,128)S(1)}, f32[2,4,4,8,128]{4,3,2,1,0:T(8,128)S(1)}, u32[]{:S(2)}, u32[]{:S(2)}) collective-permute-start(f32[2,4,4,8,128]{4,3,2,1,0:T(8,128)S(1)} %get-tuple-element.29), channel_id=1, source_target_pairs={{1,2},{2,1},{3,4},{4,3},{5,6},{6,5},{7,8},{8,7},{9,10},{10,9},{11,... | collective-permute-start | bytes 393224 | tf_op jit(solution)/shard_map/ppermute | solution.py:456
  11.1 8.9 %copy-start.1 = (f32[2,4,4,8,128]{4,3,2,1,0:T(8,128)}, f32[2,4,4,8,128]{4,3,2,1,0:T(8,128)S(1)}, u32[]{:S(2)}) copy-start(f32[2,4,4,8,128]{4,3,2,1,0:T(8,128)S(1)} %collective-permute-done.side_a) | copy-start | bytes 393220
  13.4 6.6 %copy-start.2 = (f32[2,4,4,8,128]{4,3,2,1,0:T(8,128)}, f32[2,4,4,8,128]{4,3,2,1,0:T(8,128)S(1)}, u32[]{:S(2)}) copy-start(f32[2,4,4,8,128]{4,3,2,1,0:T(8,128)S(1)} %collective-permute-done.1.side_b) | copy-start | bytes 393220
  13.5 5.6 %collective-permute-start.2 = (f32[288,128]{1,0:T(8,128)S(1)}, f32[288,128]{1,0:T(8,128)S(1)}, u32[]{:S(2)}, u32[]{:S(2)}) collective-permute-start(f32[288,128]{1,0:T(8,128)S(1)} %bitcast.34), channel_id=1, source_target_pairs={{0,16},{16,0},{32,48},{48,32},{64,80},{80,64},{96,112},{112,96},{1... | collective-permute-start | bytes 442376 | tf_op jit(solution)/shard_map/ppermute | solution.py:474
  15.1 4.9 %collective-permute-start.3 = (f32[288,128]{1,0:T(8,128)S(1)}, f32[288,128]{1,0:T(8,128)S(1)}, u32[]{:S(2)}, u32[]{:S(2)}) collective-permute-start(f32[288,128]{1,0:T(8,128)S(1)} %bitcast.33), channel_id=1, source_target_pairs={{16,32},{32,16},{48,64},{64,48},{80,96},{96,80},{112,128},{128,112... | collective-permute-start | bytes 442376 | tf_op jit(solution)/shard_map/ppermute | solution.py:475
  19.2 3.0 %copy-start = (f32[4,2,32,4,8,128]{5,4,3,2,1,0:T(8,128)}, f32[4,2,32,4,8,128]{5,4,3,2,1,0:T(8,128)S(1)}, u32[]{:S(2)}) copy-start(f32[4,2,32,4,8,128]{5,4,3,2,1,0:T(8,128)S(1)} %shard_map.37.fields.given) | copy-start | bytes 12582916
  19.2 3.0 %copy-start.3 = (f32[288,128]{1,0:T(8,128)}, f32[288,128]{1,0:T(8,128)S(1)}, u32[]{:S(2)}) copy-start(f32[288,128]{1,0:T(8,128)S(1)} %collective-permute-done.2.image_a) | copy-start | bytes 442372
  20.0 2.2 %copy-start.4 = (f32[288,128]{1,0:T(8,128)}, f32[288,128]{1,0:T(8,128)S(1)}, u32[]{:S(2)}) copy-start(f32[288,128]{1,0:T(8,128)S(1)} %collective-permute-done.3.image_b) | copy-start | bytes 442372
  22.2 17.3 %all-to-all-start = ((f32[16,1,128]{2,1,0:T(1,128)}), f32[16,1,128]{2,1,0:T(1,128)S(1)}, u32[]{:S(2)}, u32[]{:S(2)}) async-start(f32[16,1,128]{2,1,0:T(1,128)} %bitcast.14), calls=%async_computation | async-start | bytes 16384 | tf_op jit(solution)/shard_map/all_to_all | solution.py:493
  39.5 0.6 copy-start.6
  49.1 6.8 %copy-start.7 = (s32[128,2]{0,1:T(2,128)S(1)}, s32[128,2]{0,1:T(2,128)}, u32[]{:S(2)}) copy-start(s32[128,2]{0,1:T(2,128)} %param.4) | copy-start | bytes 3076
  49.2 23.5 %all-to-all-start.1 = ((f32[16,136,128]{2,1,0:T(8,128)}), f32[16,136,128]{2,1,0:T(8,128)S(1)}, u32[]{:S(2)}, u32[]{:S(2)}) async-start(f32[16,136,128]{2,1,0:T(8,128)} %shard_map.40), calls=%async_computation.1 | async-start | bytes 2228224 | tf_op jit(solution)/shard_map/all_to_all | solution.py:518
